TPU v7x, 128 devices: a whole 4x4x4 slice. The times are simulated.
128 devices in a mesh: sec: 32 (over y, x, core), mpo: 4 (over z).
Axes of the slice: x: 4, y: 4, z: 4, core: 2. Of those that a mesh axis runs over, the one named last changes fastest.
Arguments:
- wavefunction: bfloat16 [32, 256, 256], P('sec')
- block_dims: int32 [32], P('sec'), may hold values from 64 to 256, as said below
- left_env: bfloat16 [32, 24, 256, 256], P('sec', 'mpo'), may hold values from -0.0625 to 0.0625
- right_env: bfloat16 [32, 24, 256, 256], P('sec', 'mpo'), may hold values from -0.375 to 0.375
- task_left: int32 [32, 128], P('sec', 'mpo'), may hold values from 0 to 31, as said below
- task_term: int32 [32, 128], P('sec', 'mpo'), may hold values from 0 to 5
Outputs:
- first_product: float32 [32, 256, 256], P('sec', 'mpo')
- second_product: float32 [32, 256, 256], P('sec', 'mpo')
Inputs may be any that keep to these rules, and one draw needn't show every extreme that they name: `block_dims`: some sector reaches 256. `task_left`: within one row's block of 32 columns at most 2 entries name the same left sector, and in every such block one left sector, the same for all blocks, is named exactly 2 times.
All inputs are finite; a program needn't handle non-finite values.
Results may differ from a plain program's by a relative error of at most 0.005.
Values may be sent and summed in bfloat16 or wider, within the bound.
No kernel may reach another device: no remote copies, remote signals or barrier semaphores. Data moves between devices by JAX's collectives and lax.ppermute only.
A program may use at most 128 MiB of HBM per device.

v0:
```python
import jax
import jax.numpy as jnp
from jax import lax
from jax.sharding import PartitionSpec as P

epsilon = 1e-06


def body(wavefunction, block_dims, left_env, right_env, task_left, task_term):
    block_size = wavefunction.shape[1]
    sector_count = lax.axis_size("sec")
    group_count = lax.axis_size("mpo")
    group_index = lax.axis_index("mpo")
    task_count = task_left.shape[1]
    capacity = max(2, task_count // sector_count + 1)
    slot_count = sector_count * capacity
    share_size = block_size // group_count
    positions = jnp.arange(block_size, dtype=jnp.int32)
    live_dim = block_dims[0]
    live_mask = (positions[:, None] < live_dim) & (positions[None, :] < live_dim)
    psi_live = jnp.where(live_mask, wavefunction[0], jnp.zeros_like(wavefunction[0]))
    targets = task_left[0]
    term_ids = task_term[0]
    onehot = (targets[:, None] == jnp.arange(sector_count, dtype=jnp.int32)[None, :]).astype(
        jnp.int32
    )
    earlier = jnp.cumsum(onehot, axis=0) - onehot
    rank_of = jnp.sum(earlier * onehot, axis=1)
    slot_of = targets * capacity + rank_of
    matches = slot_of[:, None] == jnp.arange(slot_count, dtype=jnp.int32)[None, :]
    filled = jnp.any(matches, axis=0)
    slot_term = jnp.where(filled, jnp.sum(jnp.where(matches, term_ids[:, None], 0), axis=0), -1)
    slot_terms = slot_term.reshape(sector_count, capacity)
    own_env = right_env[0]
    own_left = left_env[0]

    def apply_hamiltonian(vector):
        everyone = lax.all_gather(vector[None], "sec", axis=0, tiled=True)
        picked = jnp.where(
            filled[:, None, None], own_env[jnp.maximum(slot_term, 0)], jnp.zeros((), jnp.bfloat16)
        )
        picked = picked.reshape(sector_count, capacity, block_size, block_size)
        envs_in, terms_in = (
            lax.all_to_all(picked, "sec", split_axis=0, concat_axis=0, tiled=True),
            lax.all_to_all(slot_terms, "sec", split_axis=0, concat_axis=0, tiled=True),
        )
        blocks = jnp.einsum(
            "pij,pcjk->pcik", everyone, envs_in, preferred_element_type=jnp.float32
        ).astype(jnp.bfloat16)
        left_blocks = own_left[jnp.maximum(terms_in, 0)]
        return jnp.einsum("pcij,pcjk->ik", left_blocks, blocks, preferred_element_type=jnp.float32)

    def collect_terms(partial_value):
        whole_block = lax.psum(partial_value, "mpo")
        return jnp.where(live_mask, whole_block, jnp.float32(0.0))

    first_result = collect_terms(apply_hamiltonian(psi_live))
    square_sum = lax.psum(jnp.sum(first_result * first_result), "sec")
    inverse_rms = lax.rsqrt(square_sum / (sector_count * block_size * block_size) + epsilon)
    new_basis = (first_result * inverse_rms).astype(jnp.bfloat16)
    second_result = collect_terms(apply_hamiltonian(new_basis))
    first_product = lax.dynamic_slice_in_dim(first_result, group_index * share_size, share_size, 0)
    second_product = lax.dynamic_slice_in_dim(
        second_result, group_index * share_size, share_size, 0
    )
    return (first_product[None], second_product[None])


def solution(mesh):
    in_specs = (
        P("sec", None, None),
        P("sec"),
        P("sec", "mpo", None, None),
        P("sec", "mpo", None, None),
        P("sec", "mpo"),
        P("sec", "mpo"),
    )
    out_specs = (P("sec", "mpo", None), P("sec", "mpo", None))
    return jax.shard_map(body, mesh=mesh, in_specs=in_specs, out_specs=out_specs, check_vma=False)
```

profile of v0, /device:TPU:0, one launch (start us, length us, event | category | flops | bytes accessed | tf_op | source)
XLA Modules:
  0.0 391.6 jit_solution(9670623709227387112)
XLA Ops:
  7.2 0.8 fusion.40
  8.0 0.8 select_reduce_fusion.1
  8.9 0.7 multiply_add_fusion
  9.6 0.7 select_reduce_fusion
  10.4 0.7 select_n.55
  11.1 7.4 %all-to-all-start = ((s32[32,1,2]{2,1,0:T(1,128)}), s32[32,1,2]{2,1,0:T(1,128)S(1)}, u32[]{:S(2)}, u32[]{:S(2)}) async-start(s32[32,1,2]{2,1,0:T(1,128)} %bitcast.4), calls=%async_computation | async-start | bytes 32768 | tf_op jit(solution)/shard_map/all_to_all | solution.py:45
  19.3 5.4 %gather_fusion.1 = bf16[64,256,256]{2,1,0:T(8,128)(2,1)} fusion(bf16[6,256,256]{2,1,0:T(8,128)(2,1)S(1)} %bitcast.42, s32[1024]{0:T(1024)S(1)} %pad_clamp_fusion), kind=kCustom, calls=%fused_computation.1 | custom fusion | bytes 16777472 | tf_op jit(solution)/shard_map/gather | solution.py:40
  24.7 7.3 %broadcast_select_fusion = bf16[32,2,256,256]{3,2,1,0:T(8,128)(2,1)} fusion(bf16[32,2,256,256]{3,2,1,0:T(8,128)(2,1)} %bitcast.44, pred[32,2]{1,0:T(8,128)(4,1)S(1)} %broadcast_in_dim.69), kind=kLoop, calls=%fused_computation.8 | loop fusion | flops 4194304 | bytes 16777280 | tf_op jit(solution)/shard_map/jit(_where)/select_n | solution.py:39
  32.0 0.8 and_select_fusion
  32.7 11.9 %copy.34 = bf16[32,2,256,256]{2,3,1,0:T(8,128)(2,1)} copy(bf16[32,2,256,256]{3,2,1,0:T(8,128)(2,1)} %broadcast_select_fusion) | data formatting | bytes 16777216 | tf_op jit(solution)/shard_map/jit(_where)/select_n | solution.py:39
  44.6 7.6 %all-to-all-start.1 = ((bf16[32,2,256,256]{2,3,1,0:T(8,128)(2,1)}), bf16[32,2,256,256]{2,3,1,0:T(8,128)(2,1)}, u32[]{:S(2)}, u32[]{:S(2)}) async-start(bf16[32,2,256,256]{2,3,1,0:T(8,128)(2,1)} %copy.34), calls=%async_computation.1 | async-start | bytes 16777216 | tf_op jit(solution)/shard_map/all_to_all | solution.py:44
  52.4 0.7 all-gather.4.cloned.1.call-update
  53.3 5.2 %gather_fusion = bf16[64,256,256]{2,1,0:T(8,128)(2,1)} fusion(bf16[6,256,256]{2,1,0:T(8,128)(2,1)S(1)} %bitcast.43, s32[1024]{0:T(1024)S(1)} %pad_clamp_fusion.1), kind=kCustom, calls=%fused_computation | custom fusion | bytes 16777472 | tf_op jit(solution)/shard_map/gather | solution.py:50
  58.5 108.4 %all-to-all-done.1 = bf16[32,2,256,256]{2,3,1,0:T(8,128)(2,1)} async-done(((bf16[32,2,256,256]{2,3,1,0:T(8,128)(2,1)}), bf16[32,2,256,256]{2,3,1,0:T(8,128)(2,1)}, u32[]{:S(2)}, u32[]{:S(2)}) %all-to-all-start.1) | async-done | bytes 8388640 | tf_op jit(solution)/shard_map/all_to_all | solution.py:44
  166.9 12.0 %fusion.22 = f32[256,256]{1,0:T(8,128)} fusion(bf16[32,2,256,256]{2,3,1,0:T(8,128)(2,1)} %all-to-all-done.1, bf16[32,256,256]{2,1,0:T(8,128)(2,1)} %all-gather.4.cloned.1.call-done, bf16[32,2,256,256]{3,2,1,0:T(8,128)(2,1)} %bitcast.45), kind=kOutput, calls=%fused_computation.16 | convolution fusion | flops 4299161600 | bytes 21233664 | tf_op jit(solution)/shard_map/pcij,pcjk->ik/dot_general | solution.py:51
  179.0 40.8 %all-reduce.3.cloned.1.call-done = f32[256,256]{1,0:T(8,128)} async-done(((f32[256,256]{1,0:T(8,128)}), f32[256,256]{1,0:T(8,128)}) %all-reduce.3.cloned.1.call-update) | async-done | bytes 262160 | tf_op jit(solution)/shard_map/psum | solution.py:54
  219.8 1.7 multiply_reduce_fusion
  221.5 65.5 %psum.22 = f32[]{:T(128)} all-reduce(f32[]{:T(128)} %get-tuple-element.2), channel_id=1, replica_groups=mesh['sec'=32,'mpo'=4] {'sec'}, use_global_device_ids=true, to_apply=%region_6.7 | all-reduce | flops 1 | bytes 8 | tf_op jit(solution)/shard_map/psum | solution.py:58
  287.6 0.7 multiply_convert_fusion
  288.3 41.7 %all-gather.6.cloned.1.call-done = bf16[8192,256]{1,0:T(8,128)(2,1)} async-done(((bf16[256,256]{1,0:T(8,128)(2,1)}), bf16[8192,256]{1,0:T(8,128)(2,1)}) %all-gather.6.cloned.1.call-update) | async-done | bytes 4194320 | tf_op jit(solution)/shard_map/all_gather | solution.py:38
  330.1 12.0 %fusion.31 = f32[256,256]{1,0:T(8,128)} fusion(bf16[32,256,256,1]{2,1,0,3:T(8,128)(2,1)} %bitcast.49, bf16[32,2,256,256]{2,3,1,0:T(8,128)(2,1)} %all-to-all-done.1, bf16[32,2,256,256]{3,2,1,0:T(8,128)(2,1)} %bitcast.46), kind=kOutput, calls=%fused_computation.17 | convolution fusion | flops 4299161600 | bytes 21233664 | tf_op jit(solution)/shard_map/pcij,pcjk->ik/dot_general | solution.py:51
  342.2 0.6 dynamic-slice_bitcast_fusion
  342.8 40.7 %all-reduce.5.cloned.1.call-done = f32[256,256]{1,0:T(8,128)} async-done(((f32[256,256]{1,0:T(8,128)}), f32[256,256]{1,0:T(8,128)}) %all-reduce.5.cloned.1.call-update) | async-done | bytes 262160 | tf_op jit(solution)/shard_map/psum | solution.py:54
  383.6 1.5 fusion.38
  (25 shorter events, 0.8 us)
Async XLA Ops:
  7.2 12.1 %copy-start = (bf16[1,6,256,256]{3,2,1,0:T(8,128)(2,1)S(1)}, bf16[1,6,256,256]{3,2,1,0:T(8,128)(2,1)}, u32[]{:S(2)}) copy-start(bf16[1,6,256,256]{3,2,1,0:T(8,128)(2,1)} %param.9) | copy-start | bytes 2359300
  11.1 33.5 %all-to-all-start = ((s32[32,1,2]{2,1,0:T(1,128)}), s32[32,1,2]{2,1,0:T(1,128)S(1)}, u32[]{:S(2)}, u32[]{:S(2)}) async-start(s32[32,1,2]{2,1,0:T(1,128)} %bitcast.4), calls=%async_computation | async-start | bytes 32768 | tf_op jit(solution)/shard_map/all_to_all | solution.py:45
  24.7 7.3 %copy-start.2 = (bf16[1,256,256]{2,1,0:T(8,128)(2,1)S(1)}, bf16[1,256,256]{2,1,0:T(8,128)(2,1)}, u32[]{:S(2)}) copy-start(bf16[1,256,256]{2,1,0:T(8,128)(2,1)} %param.6) | copy-start | bytes 393220
  44.6 8.6 %copy-start.1 = (bf16[1,6,256,256]{3,2,1,0:T(8,128)(2,1)S(1)}, bf16[1,6,256,256]{3,2,1,0:T(8,128)(2,1)}, u32[]{:S(2)}) copy-start(bf16[1,6,256,256]{3,2,1,0:T(8,128)(2,1)} %param.8) | copy-start | bytes 2359300
  44.6 122.3 %all-to-all-start.1 = ((bf16[32,2,256,256]{2,3,1,0:T(8,128)(2,1)}), bf16[32,2,256,256]{2,3,1,0:T(8,128)(2,1)}, u32[]{:S(2)}, u32[]{:S(2)}) async-start(bf16[32,2,256,256]{2,3,1,0:T(8,128)(2,1)} %copy.34), calls=%async_computation.1 | async-start | bytes 16777216 | tf_op jit(solution)/shard_map/all_to_all | solution.py:44
  52.3 114.6 %all-gather.4.cloned.1.call-start = ((), (), s32[]{:S(2)}) async-start(), calls=%async_computation.2 | async-start | bytes 4325376 | tf_op jit(solution)/shard_map/all_gather | solution.py:38
  53.0 166.7 %all-reduce.3.cloned.1.call-start = ((), (), s32[]{:S(2)}) async-start(), calls=%async_computation.3 | async-start | bytes 524288 | tf_op jit(solution)/shard_map/psum | solution.py:54
  178.9 151.1 %all-gather.6.cloned.1.call-start = ((), (), s32[]{:S(2)}) async-start(), calls=%async_computation.5 | async-start | bytes 4325376 | tf_op jit(solution)/shard_map/all_gather | solution.py:38
  288.3 95.3 %all-reduce.5.cloned.1.call-start = ((), (), s32[]{:S(2)}) async-start(), calls=%async_computation.4 | async-start | bytes 524288 | tf_op jit(solution)/shard_map/psum | solution.py:54
Sparse Core Ops, SparseCore 0:
  55.4 108.2 all-gather.3
  179.1 40.6 all-reduce.2
  288.4 41.6 all-gather.5
  342.2 41.3 all-reduce.4
where the time goes:
time: 392 us
  waiting for transfers between devices  232 us (59%)
  blocking collectives  65.5 us (17%)
  local copies, waits for them, and re-layouts  24.1 us (6%)
  matrix products  23.9 us (6%)
  other arithmetic  15.2 us (4%)
  starting transfers between devices  15.2 us (4%)
  between operations  15.2 us (4%)
    all_to_all x1, waiting for transfers between devices, apply_hamiltonian(): lax.all_to_all(picked, 'sec', split_axis=0, concat_axis=0, tiled=True)  108 us
    psum x2, waiting for transfers between devices, collect_terms(): whole_block = lax.psum(partial_value, 'mpo')  81.5 us
    psum x1, blocking collectives, body(): square_sum = lax.psum(jnp.sum(first_result * first_result), 'sec')  65.5 us
    all_gather x2, waiting for transfers between devices, apply_hamiltonian(): everyone = lax.all_gather(vector[None], 'sec', axis=0, tiled=True)  41.7 us
    dot_general x2, matrix products, apply_hamiltonian(): jnp.einsum('pcij,pcjk->ik', left_blocks, blocks, preferred_element_type=j...  23.9 us
    select_n x1, local copies, waits for them, and re-layouts, apply_hamiltonian(): jnp.where(filled[:, None, None], own_env[jnp.maximum(slot_term, 0)], jnp....  11.9 us
  transfers between devices with their start and end apart: 6, of which 4 were waited for; matrix products, arithmetic and copies ran while one was open for 8% of the time, Pallas kernels for 0%

commit v1 on v0

v1 whole, which is shorter than its diff:
```python
import jax
import jax.numpy as jnp
from jax import lax
from jax.experimental import pallas as pl
from jax.experimental.pallas import tpu as pltpu
from jax.sharding import PartitionSpec as P

BLOCK = 256
SECTORS = 32
GROUPS = 4
TERMS = 6
HALF_TERMS = 3
TASKS = 32
SLAB = 16
SLABS = BLOCK // SLAB
SHARE = BLOCK // GROUPS
LANES = 128
DATA_ROWS = HALF_TERMS * 2 * SLAB
SIDE_ROWS = 16
MIX = SECTORS * SLAB
EPSILON = 1e-06
LIFT = 512.0

F32 = jnp.float32
BF16 = jnp.bfloat16
VMEM = pl.BlockSpec(memory_space=pltpu.VMEM)
SMEM = pl.BlockSpec(memory_space=pltpu.SMEM)
PARAMS = pltpu.CompilerParams(vmem_limit_bytes=48 * 1024 * 1024)


def store_carried(vector, right_ref, out_ref):
    for term in range(TERMS):
        half, place = term // HALF_TERMS, term % HALF_TERMS
        carried = jnp.dot(vector, right_ref[0, term], preferred_element_type=F32).astype(BF16)
        for side in range(2):
            row = (place * 2 + side) * SLAB
            part = carried[:, side * LANES : (side + 1) * LANES].reshape(SLABS, SLAB, LANES)
            out_ref[:, half, row : row + SLAB, :] = part


def first_carry_kernel(dims_ref, vector_ref, right_ref, left_ref, term_ref, out_ref):
    live = dims_ref[0]
    rows = lax.broadcasted_iota(jnp.int32, (BLOCK, BLOCK), 0)
    cols = lax.broadcasted_iota(jnp.int32, (BLOCK, BLOCK), 1)
    vector = jnp.where((rows < live) & (cols < live), vector_ref[0].astype(F32), 0.0).astype(BF16)
    store_carried(vector, right_ref, out_ref)
    targets = left_ref[...]
    terms = term_ref[...]
    for half in range(2):
        place = terms - half * HALF_TERMS
        inside = (place >= 0) & (place < HALF_TERMS)
        code = jnp.where(inside, targets + place * SECTORS, 255).astype(F32)
        code = jnp.broadcast_to(code, (SIDE_ROWS, TASKS)).astype(BF16)
        for slab in range(SLABS):
            out_ref[slab, half, DATA_ROWS:, :] = jnp.zeros((SIDE_ROWS, LANES), BF16)
            out_ref[slab, half, DATA_ROWS:, :TASKS] = code


def first_carry(dims, vector, right, left, term):
    return pl.pallas_call(
        first_carry_kernel,
        out_shape=jax.ShapeDtypeStruct((SLABS, 2, DATA_ROWS + SIDE_ROWS, LANES), BF16),
        in_specs=[SMEM, VMEM, VMEM, VMEM, VMEM],
        out_specs=VMEM,
        compiler_params=PARAMS,
        name="first_carry",
    )(dims, vector, right, left, term)


def mix_with(weights_ref, in_ref, out_ref, scale):
    for place in range(HALF_TERMS):
        parts = []
        for side in range(2):
            row = (place * 2 + side) * SLAB
            parts.append(in_ref[:, row : row + SLAB, :].reshape(MIX, LANES))
        mixed = jnp.dot(
            weights_ref[place], jnp.concatenate(parts, axis=1), preferred_element_type=F32
        )
        if scale is not None:
            mixed = jnp.where(scale > 0.0, mixed * scale, 0.0)
        mixed = mixed.astype(BF16).reshape(SECTORS, SLAB, BLOCK)
        out_ref[:, place * SLAB : (place + 1) * SLAB, :] = mixed


def first_mix_kernel(in_ref, out_ref, weights_ref):
    codes = in_ref[:, DATA_ROWS : DATA_ROWS + SIDE_ROWS, :].astype(F32)[:, 0, :]
    lanes = lax.broadcasted_iota(jnp.int32, (SECTORS, LANES), 1).astype(F32)
    counts = jnp.zeros((SECTORS, LANES), F32)
    for task in range(TASKS):
        counts += jnp.where(codes[:, task : task + 1] == lanes, 1.0, 0.0)
    counts = counts.astype(BF16)
    wide_row = lax.broadcasted_iota(jnp.int32, (MIX, LANES), 0) // SLAB
    wide_col = lax.broadcasted_iota(jnp.int32, (MIX, LANES), 1)
    spread = (
        lax.broadcasted_iota(jnp.int32, (SECTORS, MIX), 0)
        == lax.broadcasted_iota(jnp.int32, (SECTORS, MIX), 1) // SLAB
    )
    spread = jnp.where(spread, 1.0, 0.0).astype(BF16)
    same_row = (
        lax.broadcasted_iota(jnp.int32, (MIX, MIX), 0) % SLAB
        == lax.broadcasted_iota(jnp.int32, (MIX, MIX), 1) % SLAB
    )
    for place in range(HALF_TERMS):
        pick = jnp.where(wide_row + place * SECTORS == wide_col, 1.0, 0.0).astype(BF16)
        tall = lax.dot_general(pick, counts, (((1,), (1,)), ((), ())), preferred_element_type=F32)
        full = jnp.dot(tall.astype(BF16), spread, preferred_element_type=F32)
        weights_ref[place] = jnp.where(same_row, full, 0.0).astype(BF16)
    mix_with(weights_ref, in_ref, out_ref, None)


def first_mix(received):
    return pl.pallas_call(
        first_mix_kernel,
        out_shape=(
            jax.ShapeDtypeStruct((SECTORS, HALF_TERMS * SLAB, BLOCK), BF16),
            jax.ShapeDtypeStruct((HALF_TERMS, MIX, MIX), BF16),
        ),
        in_specs=[VMEM],
        out_specs=(VMEM, VMEM),
        compiler_params=PARAMS,
        name="first_mix",
    )(received)


def second_mix_kernel(in_ref, weights_ref, out_ref):
    pieces = in_ref[:, DATA_ROWS : DATA_ROWS + SIDE_ROWS, :].astype(F32)
    mean = jnp.sum(pieces, keepdims=True)[0]
    inverse_rms = lax.rsqrt(mean + EPSILON) * (1.0 / LIFT)
    mix_with(weights_ref, in_ref, out_ref, inverse_rms)


def second_mix(received, weights):
    return pl.pallas_call(
        second_mix_kernel,
        out_shape=jax.ShapeDtypeStruct((SECTORS, HALF_TERMS * SLAB, BLOCK), BF16),
        in_specs=[VMEM, VMEM],
        out_specs=VMEM,
        compiler_params=PARAMS,
        name="second_mix",
    )(received, weights)


def left_kernel(group_ref, in_ref, left_ref, *refs):
    *out_refs, total = refs
    value = jnp.zeros((BLOCK, BLOCK), F32)
    for term in range(TERMS):
        half, place = term // HALF_TERMS, term % HALF_TERMS
        mixed = in_ref[:, half, place * SLAB : (place + 1) * SLAB, :].reshape(BLOCK, BLOCK)
        value += jnp.dot(left_ref[0, term], mixed, preferred_element_type=F32)
    total[...] = value
    for step in range(GROUPS):
        owner = lax.rem(group_ref[0] + step, GROUPS)
        out_refs[step][...] = total[pl.ds(pl.multiple_of(owner * SHARE, SHARE), SHARE), :]


def apply_left(group, received, left_env):
    share = jax.ShapeDtypeStruct((SHARE, BLOCK), F32)
    return pl.pallas_call(
        left_kernel,
        out_shape=(share,) * GROUPS,
        in_specs=[SMEM, VMEM, VMEM],
        out_specs=(VMEM,) * GROUPS,
        scratch_shapes=[pltpu.VMEM((BLOCK, BLOCK), F32)],
        compiler_params=PARAMS,
        name="apply_left",
    )(group, received.reshape(SLABS, 2, HALF_TERMS * SLAB, BLOCK), left_env)


def live_sum(group_ref, dims_ref, part_refs):
    live = dims_ref[0]
    rows = lax.broadcasted_iota(jnp.int32, (SHARE, BLOCK), 0) + group_ref[0] * SHARE
    cols = lax.broadcasted_iota(jnp.int32, (SHARE, BLOCK), 1)
    value = (part_refs[0][...] + part_refs[1][...]) + (part_refs[2][...] + part_refs[3][...])
    return jnp.where((rows < live) & (cols < live), value, 0.0)


def first_sum_kernel(group_ref, dims_ref, *refs):
    *part_refs, out_ref, basis_ref = refs
    value = live_sum(group_ref, dims_ref, part_refs)
    out_ref[0] = value
    basis_ref[:SHARE, :] = (value * LIFT).astype(BF16)
    mean = jnp.sum(value * value, keepdims=True) * (1.0 / (SECTORS * BLOCK * BLOCK))
    high = mean.astype(BF16)
    rest = jnp.where(mean < jnp.inf, mean - high.astype(F32), 0.0)
    middle = rest.astype(BF16)
    low = (rest - middle.astype(F32)).astype(BF16)
    lane = lax.broadcasted_iota(jnp.int32, (SIDE_ROWS, BLOCK), 1)
    row = lax.broadcasted_iota(jnp.int32, (SIDE_ROWS, BLOCK), 0)
    pieces = jnp.where(lane == 0, high.astype(F32), 0.0)
    pieces = jnp.where(lane == 1, middle.astype(F32), pieces)
    pieces = jnp.where(lane == 2, low.astype(F32), pieces)
    basis_ref[SHARE:, :] = jnp.where(row == 0, pieces, 0.0).astype(BF16)


def first_sum(group, dims, parts):
    return pl.pallas_call(
        first_sum_kernel,
        out_shape=(
            jax.ShapeDtypeStruct((1, SHARE, BLOCK), F32),
            jax.ShapeDtypeStruct((SHARE + SIDE_ROWS, BLOCK), BF16),
        ),
        in_specs=[SMEM, SMEM] + [VMEM] * GROUPS,
        out_specs=(VMEM, VMEM),
        compiler_params=PARAMS,
        name="first_sum",
    )(group, dims, *parts)


def second_sum_kernel(group_ref, dims_ref, *refs):
    *part_refs, out_ref = refs
    out_ref[0] = live_sum(group_ref, dims_ref, part_refs)


def second_sum(group, dims, parts):
    return pl.pallas_call(
        second_sum_kernel,
        out_shape=jax.ShapeDtypeStruct((1, SHARE, BLOCK), F32),
        in_specs=[SMEM, SMEM] + [VMEM] * GROUPS,
        out_specs=VMEM,
        compiler_params=PARAMS,
        name="second_sum",
    )(group, dims, *parts)


def second_carry_kernel(group_ref, right_ref, *refs):
    *part_refs, out_ref, vector_ref = refs
    pieces = jnp.zeros((SIDE_ROWS, LANES), F32)
    lane = lax.broadcasted_iota(jnp.int32, (SIDE_ROWS, LANES), 1)
    for step in range(GROUPS):
        owner = lax.rem(group_ref[0] + GROUPS - step, GROUPS)
        rows = pl.ds(pl.multiple_of(owner * SHARE, SHARE), SHARE)
        vector_ref[rows, :] = part_refs[step][:SHARE, :]
        got = part_refs[step][SHARE:, :LANES].astype(F32)
        pieces += got if step == 0 else pltpu.roll(got, 3 * step, 1)
    store_carried(vector_ref[...], right_ref, out_ref)
    pieces = jnp.where(lane < 3 * GROUPS, pieces, 0.0).astype(BF16)
    for slab in range(SLABS):
        for half in range(2):
            out_ref[slab, half, DATA_ROWS:, :] = pieces


def second_carry(group, right, parts):
    return pl.pallas_call(
        second_carry_kernel,
        out_shape=jax.ShapeDtypeStruct((SLABS, 2, DATA_ROWS + SIDE_ROWS, LANES), BF16),
        in_specs=[SMEM, VMEM] + [VMEM] * GROUPS,
        out_specs=VMEM,
        scratch_shapes=[pltpu.VMEM((BLOCK, BLOCK), BF16)],
        compiler_params=PARAMS,
        name="second_carry",
    )(group, right, *parts)


def exchange(messages):
    messages = messages.reshape((SECTORS,) + messages.shape[-2:])
    return lax.all_to_all(messages, "sec", split_axis=0, concat_axis=0, tiled=True)


def shift(value, step):
    pairs = [(group, (group + step) % GROUPS) for group in range(GROUPS)]
    return lax.ppermute(value, "mpo", pairs)


def body(wavefunction, block_dims, left_env, right_env, task_left, task_term):
    group = lax.axis_index("mpo").astype(jnp.int32).reshape(1)
    carried = first_carry(block_dims, wavefunction, right_env, task_left, task_term)
    mixed, weights = first_mix(exchange(carried))
    parts = apply_left(group, exchange(mixed), left_env)
    parts = [parts[0]] + [shift(parts[step], step) for step in range(1, GROUPS)]
    first_product, basis = first_sum(group, block_dims, parts)
    parts = [basis] + [shift(basis, step) for step in range(1, GROUPS)]
    carried = second_carry(group, right_env, parts)
    mixed = second_mix(exchange(carried), weights)
    parts = apply_left(group, exchange(mixed), left_env)
    parts = [parts[0]] + [shift(parts[step], step) for step in range(1, GROUPS)]
    second_product = second_sum(group, block_dims, parts)
    return (first_product, second_product)


def solution(mesh):
    in_specs = (
        P("sec", None, None),
        P("sec"),
        P("sec", "mpo", None, None),
        P("sec", "mpo", None, None),
        P("sec", "mpo"),
        P("sec", "mpo"),
    )
    out_specs = (P("sec", "mpo", None), P("sec", "mpo", None))
    return jax.shard_map(body, mesh=mesh, in_specs=in_specs, out_specs=out_specs, check_vma=False)
```

time: 392 us -> 117 us (0.30)
  waiting for transfers between devices: 232 us -> 25.6 us
  matrix products: 23.9 us -> 0 us
  local copies, waits for them, and re-layouts: 24.1 us -> 4.52 us
  other arithmetic: 15.2 us -> 0 us
  between operations: 15.2 us -> 1.36 us
  Pallas kernels: 0 us -> 6.79 us
  blocking collectives: 65.5 us -> 60.3 us
    all_to_all x2 -> x1, waiting for transfers between devices: 108 us -> 14.6 us  [exchange(): lax.all_to_all(messages, 'sec', split_axis=0, concat_axis=0, tiled=True)]
    psum x2 -> x0, waiting for transfers between devices: 81.5 us -> none  [collect_terms(): whole_block = lax.psum(partial_value, 'mpo')]
    psum x1 -> x0, blocking collectives: 65.5 us -> none  [body(): square_sum = lax.psum(jnp.sum(first_result * first_result), 'sec')]
    all_to_all x0 -> x3, blocking collectives: none -> 60.3 us  [exchange(): lax.all_to_all(messages, 'sec', split_axis=0, concat_axis=0, tiled=True)]
    all_gather x2 -> x0, waiting for transfers between devices: 41.7 us -> none  [apply_hamiltonian(): everyone = lax.all_gather(vector[None], 'sec', axis=0, tiled=True)]
    dot_general x2 -> x0, matrix products: 23.9 us -> none  [apply_hamiltonian(): jnp.einsum('pcij,pcjk->ik', left_blocks, blocks, preferred_element_type=j...]
    ppermute x0 -> x9, starting transfers between devices: none -> 14 us  [shift(): return lax.ppermute(value, 'mpo', pairs)]
    select_n x2 -> x0, local copies, waits for them, and re-layouts: 12.6 us -> none  [the longest x1 11.9 us: apply_hamiltonian(): jnp.where(filled[:, None, None], own_env[jnp.maximum(slot_term, 0)], jnp....]
  transfers between devices with their start and end apart: 6 -> 10, of which waited for: 4 -> 8; matrix products, arithmetic and copies ran while one was open for 8% -> 0% of each run, Pallas kernels for 0% -> 0%
where the time goes in v1:
time: 117 us
  blocking collectives  60.3 us (52%)
  waiting for transfers between devices  25.6 us (22%)
  starting transfers between devices  18 us (15%)
  Pallas kernels  6.79 us (6%)
  local copies, waits for them, and re-layouts  4.52 us (4%)
  between operations  1.36 us (1%)
    all_to_all x3, blocking collectives, exchange(): lax.all_to_all(messages, 'sec', split_axis=0, concat_axis=0, tiled=True)  60.3 us
    all_to_all x1, waiting for transfers between devices, exchange(): lax.all_to_all(messages, 'sec', split_axis=0, concat_axis=0, tiled=True)  14.6 us
    ppermute x9, starting transfers between devices, shift(): return lax.ppermute(value, 'mpo', pairs)  14 us
    ppermute x9, waiting for transfers between devices, shift(): return lax.ppermute(value, 'mpo', pairs)  11 us
    unnamed x16, local copies, waits for them, and re-layouts  4.52 us
    all_to_all x1, starting transfers between devices, exchange(): lax.all_to_all(messages, 'sec', split_axis=0, concat_axis=0, tiled=True)  4.04 us
    pallas_call x1, Pallas kernels, first_mix(): pl.pallas_call(first_mix_kernel, out_shape=(jax.ShapeDtypeStruct((SECTORS...  3.35 us
  transfers between devices with their start and end apart: 10, of which 8 were waited for; matrix products, arithmetic and copies ran while one was open for 0% of the time, Pallas kernels for 0%

profile of v1, /device:TPU:0, one launch (start us, length us, event | category | flops | bytes accessed | tf_op | source)
XLA Modules:
  0.0 116.6 jit_solution(7760832592614359179)
XLA Ops:
  1.3 1.1 copy-done.1
  2.4 0.9 copy-done.5
  3.3 0.7 copy-done.6
  4.0 0.7 copy-done.7
  5.0 23.1 %all_to_all.20.in_ref = bf16[32,112,128]{2,1,0:T(8,128)(2,1)S(1)} all-to-all(bf16[32,112,128]{2,1,0:T(8,128)(2,1)S(1)} %bitcast.6), channel_id=1, replica_groups=mesh['sec'=32,'mpo'=4] {'sec'}, dimensions={0} | all-to-all | bytes 1835008 | tf_op jit(solution)/shard_map/all_to_all | solution.py:256
  28.1 3.3 %first_mix.1 = (bf16[32,48,256]{2,1,0:T(8,128)(2,1)}, bf16[3,512,512]{2,1,0:T(8,128)(2,1)S(1)}) custom-call(bf16[32,112,128]{2,1,0:T(8,128)(2,1)S(1)} %all_to_all.20.in_ref), custom_call_target="tpu_custom_call" | custom-call | tf_op jit(solution)/shard_map/first_mix/pallas_call | solution.py:112
  31.5 1.2 copy-done.3
  32.6 4.0 %all-to-all-start.1 = ((bf16[32,48,256]{2,1,0:T(8,128)(2,1)}), bf16[32,48,256]{2,1,0:T(8,128)(2,1)S(1)}, u32[]{:S(2)}, u32[]{:S(2)}) async-start(bf16[32,48,256]{2,1,0:T(8,128)(2,1)} %get-tuple-element.14), calls=%async_computation.1 | async-start | bytes 1572864 | tf_op jit(solution)/shard_map/all_to_all | solution.py:256
  36.7 14.6 %all-to-all-done.1 = bf16[32,48,256]{2,1,0:T(8,128)(2,1)S(1)} async-done(((bf16[32,48,256]{2,1,0:T(8,128)(2,1)}), bf16[32,48,256]{2,1,0:T(8,128)(2,1)S(1)}, u32[]{:S(2)}, u32[]{:S(2)}) %all-to-all-start.1) | async-done | bytes 786464 | tf_op jit(solution)/shard_map/all_to_all | solution.py:256
  51.7 2.0 %collective-permute-start = (f32[64,256]{1,0:T(8,128)S(1)}, f32[64,256]{1,0:T(8,128)S(1)}, u32[]{:S(2)}, u32[]{:S(2)}) collective-permute-start(f32[64,256]{1,0:T(8,128)S(1)} %get-tuple-element.16), channel_id=1, source_target_pairs={{0,1},{1,2},{2,3},{3,0},{4,5},{5,6},{6,7},{7,4},{8,9},{9,10},{10,1... | collective-permute-start | bytes 196616 | tf_op jit(solution)/shard_map/ppermute | solution.py:261
  53.7 3.6 %collective-permute-start.1 = (f32[64,256]{1,0:T(8,128)S(1)}, f32[64,256]{1,0:T(8,128)S(1)}, u32[]{:S(2)}, u32[]{:S(2)}) collective-permute-start(f32[64,256]{1,0:T(8,128)S(1)} %get-tuple-element.17), channel_id=1, source_target_pairs={{0,2},{1,3},{2,0},{3,1},{4,6},{5,7},{6,4},{7,5},{8,10},{9,11},{10,... | collective-permute-start | bytes 196616 | tf_op jit(solution)/shard_map/ppermute | solution.py:261
  57.2 1.0 collective-permute-start.2
  58.2 2.3 %collective-permute-done.1.refs_2_ = f32[64,256]{1,0:T(8,128)S(1)} collective-permute-done((f32[64,256]{1,0:T(8,128)S(1)}, f32[64,256]{1,0:T(8,128)S(1)}, u32[]{:S(2)}, u32[]{:S(2)}) %collective-permute-start.1) | collective-permute-done | bytes 65568 | tf_op jit(solution)/shard_map/ppermute | solution.py:261
  60.5 0.9 collective-permute-done.2.refs_3_
  61.5 0.7 first_sum.1
  62.2 2.2 %collective-permute-start.5 = (bf16[80,256]{1,0:T(8,128)(2,1)S(1)}, bf16[80,256]{1,0:T(8,128)(2,1)S(1)}, u32[]{:S(2)}, u32[]{:S(2)}) collective-permute-start(bf16[80,256]{1,0:T(8,128)(2,1)S(1)} %get-tuple-element.20.refs_0_), channel_id=1, source_target_pairs={{0,3},{1,0},{2,1},{3,2},{4,7},{5,4},{6,5},{7,6},{8,11},{9,8},{10,9... | collective-permute-start | bytes 122888 | tf_op jit(solution)/shard_map/ppermute | solution.py:261
  64.5 0.7 collective-permute-start.3
  65.2 0.9 collective-permute-done.5.refs_3_
  66.2 3.8 %collective-permute-done.4.refs_2_ = bf16[80,256]{1,0:T(8,128)(2,1)S(1)} collective-permute-done((bf16[80,256]{1,0:T(8,128)(2,1)S(1)}, bf16[80,256]{1,0:T(8,128)(2,1)S(1)}, u32[]{:S(2)}, u32[]{:S(2)}) %collective-permute-start.4) | collective-permute-done | bytes 40992 | tf_op jit(solution)/shard_map/ppermute | solution.py:261
  70.5 19.2 %all_to_all.21.in_ref = bf16[32,112,128]{2,1,0:T(8,128)(2,1)S(1)} all-to-all(bf16[32,112,128]{2,1,0:T(8,128)(2,1)S(1)} %bitcast.5), channel_id=1, replica_groups=mesh['sec'=32,'mpo'=4] {'sec'}, dimensions={0} | all-to-all | bytes 1835008 | tf_op jit(solution)/shard_map/all_to_all | solution.py:256
  90.4 17.9 %all_to_all.22 = bf16[32,48,256]{2,1,0:T(8,128)(2,1)S(1)} all-to-all(bf16[32,48,256]{2,1,0:T(8,128)(2,1)S(1)} %second_mix.1), channel_id=1, replica_groups=mesh['sec'=32,'mpo'=4] {'sec'}, dimensions={0} | all-to-all | bytes 1572864 | tf_op jit(solution)/shard_map/all_to_all | solution.py:256
  108.8 2.1 %collective-permute-start.7 = (f32[64,256]{1,0:T(8,128)S(1)}, f32[64,256]{1,0:T(8,128)S(1)}, u32[]{:S(2)}, u32[]{:S(2)}) collective-permute-start(f32[64,256]{1,0:T(8,128)S(1)} %get-tuple-element.24), channel_id=1, source_target_pairs={{0,2},{1,3},{2,0},{3,1},{4,6},{5,7},{6,4},{7,5},{8,10},{9,11},{10,... | collective-permute-start | bytes 196616 | tf_op jit(solution)/shard_map/ppermute | solution.py:261
  110.9 2.2 %collective-permute-start.8 = (f32[64,256]{1,0:T(8,128)S(1)}, f32[64,256]{1,0:T(8,128)S(1)}, u32[]{:S(2)}, u32[]{:S(2)}) collective-permute-start(f32[64,256]{1,0:T(8,128)S(1)} %get-tuple-element.25), channel_id=1, source_target_pairs={{0,3},{1,0},{2,1},{3,2},{4,7},{5,4},{6,5},{7,6},{8,11},{9,8},{10,9... | collective-permute-start | bytes 196616 | tf_op jit(solution)/shard_map/ppermute | solution.py:261
  113.1 2.3 %collective-permute-done.6.refs_1_ = f32[64,256]{1,0:T(8,128)S(1)} collective-permute-done((f32[64,256]{1,0:T(8,128)S(1)}, f32[64,256]{1,0:T(8,128)S(1)}, u32[]{:S(2)}, u32[]{:S(2)}) %collective-permute-start.6) | collective-permute-done | bytes 65568 | tf_op jit(solution)/shard_map/ppermute | solution.py:261
  (23 shorter events, 3.8 us)
Async XLA Ops:
  1.3 1.1 copy-start.1
  2.4 0.9 copy-start.5
  3.3 0.7 copy-start.6
  4.0 0.7 copy-start.7
  28.1 23.1 %copy-start = (bf16[1,6,256,256]{3,2,1,0:T(8,128)(2,1)S(1)}, bf16[1,6,256,256]{3,2,1,0:T(8,128)(2,1)}, u32[]{:S(2)}) copy-start(bf16[1,6,256,256]{3,2,1,0:T(8,128)(2,1)} %left_ref.5) | copy-start | bytes 2359300
  31.5 1.2 copy-start.3
  32.6 37.5 %copy-start.2 = (bf16[1,6,256,256]{3,2,1,0:T(8,128)(2,1)S(1)}, bf16[1,6,256,256]{3,2,1,0:T(8,128)(2,1)}, u32[]{:S(2)}) copy-start(bf16[1,6,256,256]{3,2,1,0:T(8,128)(2,1)} %right_ref.3) | copy-start | bytes 2359300
  32.6 18.6 %all-to-all-start.1 = ((bf16[32,48,256]{2,1,0:T(8,128)(2,1)}), bf16[32,48,256]{2,1,0:T(8,128)(2,1)S(1)}, u32[]{:S(2)}, u32[]{:S(2)}) async-start(bf16[32,48,256]{2,1,0:T(8,128)(2,1)} %get-tuple-element.14), calls=%async_computation.1 | async-start | bytes 1572864 | tf_op jit(solution)/shard_map/all_to_all | solution.py:256
  51.7 6.6 %collective-permute-start = (f32[64,256]{1,0:T(8,128)S(1)}, f32[64,256]{1,0:T(8,128)S(1)}, u32[]{:S(2)}, u32[]{:S(2)}) collective-permute-start(f32[64,256]{1,0:T(8,128)S(1)} %get-tuple-element.16), channel_id=1, source_target_pairs={{0,1},{1,2},{2,3},{3,0},{4,5},{5,6},{6,7},{7,4},{8,9},{9,10},{10,1... | collective-permute-start | bytes 196616 | tf_op jit(solution)/shard_map/ppermute | solution.py:261
  53.7 6.9 %collective-permute-start.1 = (f32[64,256]{1,0:T(8,128)S(1)}, f32[64,256]{1,0:T(8,128)S(1)}, u32[]{:S(2)}, u32[]{:S(2)}) collective-permute-start(f32[64,256]{1,0:T(8,128)S(1)} %get-tuple-element.17), channel_id=1, source_target_pairs={{0,2},{1,3},{2,0},{3,1},{4,6},{5,7},{6,4},{7,5},{8,10},{9,11},{10,... | collective-permute-start | bytes 196616 | tf_op jit(solution)/shard_map/ppermute | solution.py:261
  57.2 4.3 %collective-permute-start.2 = (f32[64,256]{1,0:T(8,128)S(1)}, f32[64,256]{1,0:T(8,128)S(1)}, u32[]{:S(2)}, u32[]{:S(2)}) collective-permute-start(f32[64,256]{1,0:T(8,128)S(1)} %get-tuple-element.18), channel_id=1, source_target_pairs={{0,3},{1,0},{2,1},{3,2},{4,7},{5,4},{6,5},{7,6},{8,11},{9,8},{10,9... | collective-permute-start | bytes 196616 | tf_op jit(solution)/shard_map/ppermute | solution.py:261
  62.1 27.6 %copy-start.4 = (bf16[3,512,512]{2,1,0:T(8,128)(2,1)S(1)}, bf16[3,512,512]{2,1,0:T(8,128)(2,1)}, u32[]{:S(2)}) copy-start(bf16[3,512,512]{2,1,0:T(8,128)(2,1)} %copy-done.3) | copy-start | bytes 4718596
  62.2 4.0 %collective-permute-start.5 = (bf16[80,256]{1,0:T(8,128)(2,1)S(1)}, bf16[80,256]{1,0:T(8,128)(2,1)S(1)}, u32[]{:S(2)}, u32[]{:S(2)}) collective-permute-start(bf16[80,256]{1,0:T(8,128)(2,1)S(1)} %get-tuple-element.20.refs_0_), channel_id=1, source_target_pairs={{0,3},{1,0},{2,1},{3,2},{4,7},{5,4},{6,5},{7,6},{8,11},{9,8},{10,9... | collective-permute-start | bytes 122888 | tf_op jit(solution)/shard_map/ppermute | solution.py:261
  64.4 5.6 %collective-permute-start.4 = (bf16[80,256]{1,0:T(8,128)(2,1)S(1)}, bf16[80,256]{1,0:T(8,128)(2,1)S(1)}, u32[]{:S(2)}, u32[]{:S(2)}) collective-permute-start(bf16[80,256]{1,0:T(8,128)(2,1)S(1)} %get-tuple-element.20.refs_0_), channel_id=1, source_target_pairs={{0,2},{1,3},{2,0},{3,1},{4,6},{5,7},{6,4},{7,5},{8,10},{9,11},{10,... | collective-permute-start | bytes 122888 | tf_op jit(solution)/shard_map/ppermute | solution.py:261
  64.5 5.7 %collective-permute-start.3 = (bf16[80,256]{1,0:T(8,128)(2,1)S(1)}, bf16[80,256]{1,0:T(8,128)(2,1)S(1)}, u32[]{:S(2)}, u32[]{:S(2)}) collective-permute-start(bf16[80,256]{1,0:T(8,128)(2,1)S(1)} %get-tuple-element.20.refs_0_), channel_id=1, source_target_pairs={{0,1},{1,2},{2,3},{3,0},{4,5},{5,6},{6,7},{7,4},{8,9},{9,10},{10,1... | collective-permute-start | bytes 122888 | tf_op jit(solution)/shard_map/ppermute | solution.py:261
  108.7 6.6 %collective-permute-start.6 = (f32[64,256]{1,0:T(8,128)S(1)}, f32[64,256]{1,0:T(8,128)S(1)}, u32[]{:S(2)}, u32[]{:S(2)}) collective-permute-start(f32[64,256]{1,0:T(8,128)S(1)} %get-tuple-element.23), channel_id=1, source_target_pairs={{0,1},{1,2},{2,3},{3,0},{4,5},{5,6},{6,7},{7,4},{8,9},{9,10},{10,1... | collective-permute-start | bytes 196616 | tf_op jit(solution)/shard_map/ppermute | solution.py:261
  108.8 6.5 %collective-permute-start.7 = (f32[64,256]{1,0:T(8,128)S(1)}, f32[64,256]{1,0:T(8,128)S(1)}, u32[]{:S(2)}, u32[]{:S(2)}) collective-permute-start(f32[64,256]{1,0:T(8,128)S(1)} %get-tuple-element.24), channel_id=1, source_target_pairs={{0,2},{1,3},{2,0},{3,1},{4,6},{5,7},{6,4},{7,5},{8,10},{9,11},{10,... | collective-permute-start | bytes 196616 | tf_op jit(solution)/shard_map/ppermute | solution.py:261
  110.9 5.0 %collective-permute-start.8 = (f32[64,256]{1,0:T(8,128)S(1)}, f32[64,256]{1,0:T(8,128)S(1)}, u32[]{:S(2)}, u32[]{:S(2)}) collective-permute-start(f32[64,256]{1,0:T(8,128)S(1)} %get-tuple-element.25), channel_id=1, source_target_pairs={{0,3},{1,0},{2,1},{3,2},{4,7},{5,4},{6,5},{7,6},{8,11},{9,8},{10,9... | collective-permute-start | bytes 196616 | tf_op jit(solution)/shard_map/ppermute | solution.py:261

commit v2 on v1

v2 whole, which is shorter than its diff:
```python
import jax
import jax.numpy as jnp
from jax import lax
from jax.experimental import pallas as pl
from jax.experimental.pallas import tpu as pltpu
from jax.sharding import PartitionSpec as P

BLOCK = 256
SECTORS = 32
GROUPS = 4
TERMS = 6
HALF_TERMS = 3
TASKS = 32
SLAB = 16
SLABS = BLOCK // SLAB
SHARE = BLOCK // GROUPS
LANES = 128
DATA_ROWS = HALF_TERMS * 2 * SLAB
SIDE_ROWS = 16
MIX = SECTORS * SLAB
EPSILON = 1e-06
LIFT = 512.0

F32 = jnp.float32
BF16 = jnp.bfloat16
VMEM = pl.BlockSpec(memory_space=pltpu.VMEM)
SMEM = pl.BlockSpec(memory_space=pltpu.SMEM)
HBM = pl.BlockSpec(memory_space=pltpu.HBM)
PARAMS = pltpu.CompilerParams(vmem_limit_bytes=48 * 1024 * 1024)


def store_carried(term, carried, out_ref):
    half, place = term // HALF_TERMS, term % HALF_TERMS
    carried = carried.astype(BF16)
    for side in range(2):
        row = (place * 2 + side) * SLAB
        part = carried[:, side * LANES : (side + 1) * LANES].reshape(SLABS, SLAB, LANES)
        out_ref[:, half, row : row + SLAB, :] = part


def first_carry_kernel(
    dims_ref, group_ref, vector_hbm, right_hbm, left_hbm, term_hbm, out_ref, vector_ref, right_ref, left_ref, term_ref, sems
):
    del group_ref
    copies = [
        pltpu.make_async_copy(left_hbm, left_ref, sems.at[TERMS]),
        pltpu.make_async_copy(term_hbm, term_ref, sems.at[TERMS + 1]),
        pltpu.make_async_copy(vector_hbm, vector_ref, sems.at[TERMS + 2]),
    ]
    fetches = [
        pltpu.make_async_copy(right_hbm.at[0, term], right_ref.at[0, term], sems.at[term])
        for term in range(TERMS)
    ]
    for copy in copies + fetches:
        copy.start()
    copies[0].wait()
    copies[1].wait()
    targets = left_ref[...]
    terms = term_ref[...]
    for half in range(2):
        place = terms - half * HALF_TERMS
        inside = (place >= 0) & (place < HALF_TERMS)
        code = jnp.where(inside, targets + place * SECTORS, 255).astype(F32)
        code = jnp.broadcast_to(code, (SIDE_ROWS, TASKS)).astype(BF16)
        for slab in range(SLABS):
            out_ref[slab, half, DATA_ROWS:, :] = jnp.zeros((SIDE_ROWS, LANES), BF16)
            out_ref[slab, half, DATA_ROWS:, :TASKS] = code
    copies[2].wait()
    live = dims_ref[0]
    rows = lax.broadcasted_iota(jnp.int32, (BLOCK, BLOCK), 0)
    cols = lax.broadcasted_iota(jnp.int32, (BLOCK, BLOCK), 1)
    vector = jnp.where((rows < live) & (cols < live), vector_ref[0].astype(F32), 0.0).astype(BF16)
    for term in range(TERMS):
        fetches[term].wait()
        carried = jnp.dot(vector, right_ref[0, term], preferred_element_type=F32)
        store_carried(term, carried, out_ref)


def first_carry(dims, group, vector, right, left, term):
    return pl.pallas_call(
        first_carry_kernel,
        out_shape=jax.ShapeDtypeStruct((SLABS, 2, DATA_ROWS + SIDE_ROWS, LANES), BF16),
        in_specs=[SMEM, SMEM, HBM, HBM, HBM, HBM],
        out_specs=VMEM,
        scratch_shapes=[
            pltpu.VMEM((1, BLOCK, BLOCK), BF16),
            pltpu.VMEM((1, TERMS, BLOCK, BLOCK), BF16),
            pltpu.VMEM((1, TASKS), jnp.int32),
            pltpu.VMEM((1, TASKS), jnp.int32),
            pltpu.SemaphoreType.DMA((TERMS + 3,)),
        ],
        compiler_params=PARAMS,
        name="first_carry",
    )(dims, group, vector, right, left, term)


def mix_with(weights_ref, in_ref, out_ref, scale):
    for place in range(HALF_TERMS):
        parts = []
        for side in range(2):
            row = (place * 2 + side) * SLAB
            parts.append(in_ref[:, row : row + SLAB, :].reshape(MIX, LANES))
        mixed = jnp.dot(
            weights_ref[place], jnp.concatenate(parts, axis=1), preferred_element_type=F32
        )
        if scale is not None:
            mixed = jnp.where(scale > 0.0, mixed * scale, 0.0)
        mixed = mixed.astype(BF16).reshape(SECTORS, SLAB, BLOCK)
        out_ref[:, place * SLAB : (place + 1) * SLAB, :] = mixed


def first_mix_kernel(in_ref, out_ref, weights_ref, wide_ref):
    codes = in_ref[:, DATA_ROWS : DATA_ROWS + SIDE_ROWS, :].astype(F32)[:, 0, :]
    lanes = lax.broadcasted_iota(jnp.int32, (SECTORS, LANES), 1).astype(F32)
    counts = jnp.zeros((SECTORS, LANES), F32)
    for task in range(TASKS):
        counts += jnp.where(codes[:, task : task + 1] == lanes, 1.0, 0.0)
    counts = counts.astype(BF16)
    spread = (
        lax.broadcasted_iota(jnp.int32, (SECTORS, MIX), 0)
        == lax.broadcasted_iota(jnp.int32, (SECTORS, MIX), 1) // SLAB
    )
    spread = jnp.where(spread, 1.0, 0.0).astype(BF16)
    wide_ref[...] = lax.dot_general(
        counts, spread, (((0,), (0,)), ((), ())), preferred_element_type=F32
    )
    same_row = (
        lax.broadcasted_iota(jnp.int32, (SLAB, MIX), 0)
        == lax.broadcasted_iota(jnp.int32, (SLAB, MIX), 1) % SLAB
    )
    same_row = jnp.where(same_row, 1.0, 0.0)
    for place in range(HALF_TERMS):
        for target in range(SECTORS):
            line = place * SECTORS + target
            weights_ref[place, target * SLAB : (target + 1) * SLAB, :] = (
                same_row * wide_ref[line : line + 1, :]
            ).astype(BF16)
    mix_with(weights_ref, in_ref, out_ref, None)


def first_mix(received):
    return pl.pallas_call(
        first_mix_kernel,
        out_shape=(
            jax.ShapeDtypeStruct((SECTORS, HALF_TERMS * SLAB, BLOCK), BF16),
            jax.ShapeDtypeStruct((HALF_TERMS, MIX, MIX), BF16),
        ),
        in_specs=[VMEM],
        out_specs=(VMEM, VMEM),
        scratch_shapes=[pltpu.VMEM((LANES, MIX), F32)],
        compiler_params=PARAMS,
        name="first_mix",
    )(received)


def second_mix_kernel(in_ref, weights_ref, out_ref):
    pieces = in_ref[:, DATA_ROWS : DATA_ROWS + SIDE_ROWS, :].astype(F32)
    mean = jnp.sum(pieces, keepdims=True)[0]
    inverse_rms = lax.rsqrt(mean + EPSILON) * (1.0 / LIFT)
    mix_with(weights_ref, in_ref, out_ref, inverse_rms)


def second_mix(received, weights):
    return pl.pallas_call(
        second_mix_kernel,
        out_shape=jax.ShapeDtypeStruct((SECTORS, HALF_TERMS * SLAB, BLOCK), BF16),
        in_specs=[VMEM, VMEM],
        out_specs=VMEM,
        compiler_params=PARAMS,
        name="second_mix",
    )(received, weights)


def left_product(in_ref, left_ref):
    value = jnp.zeros((BLOCK, BLOCK), F32)
    for term in range(TERMS):
        half, place = term // HALF_TERMS, term % HALF_TERMS
        mixed = in_ref[:, half, place * SLAB : (place + 1) * SLAB, :].reshape(BLOCK, BLOCK)
        value += jnp.dot(left_ref[0, term], mixed, preferred_element_type=F32)
    return value


def first_left_kernel(in_ref, left_ref, own_ref, sent_ref):
    value = left_product(in_ref, left_ref)
    own_ref[...] = value
    sent_ref[...] = value.astype(BF16)


def first_left(received, left_env):
    return pl.pallas_call(
        first_left_kernel,
        out_shape=(
            jax.ShapeDtypeStruct((BLOCK, BLOCK), F32),
            jax.ShapeDtypeStruct((BLOCK, BLOCK), BF16),
        ),
        in_specs=[VMEM, VMEM],
        out_specs=(VMEM, VMEM),
        compiler_params=PARAMS,
        name="first_left",
    )(received.reshape(SLABS, 2, HALF_TERMS * SLAB, BLOCK), left_env)


def second_left_kernel(group_ref, in_ref, left_ref, *refs):
    *out_refs, total = refs
    total[...] = left_product(in_ref, left_ref)
    for step in range(GROUPS):
        owner = lax.rem(group_ref[0] + step, GROUPS)
        out_refs[step][...] = total[pl.ds(pl.multiple_of(owner * SHARE, SHARE), SHARE), :]


def second_left(group, received, left_env):
    share = jax.ShapeDtypeStruct((SHARE, BLOCK), F32)
    return pl.pallas_call(
        second_left_kernel,
        out_shape=(share,) * GROUPS,
        in_specs=[SMEM, VMEM, VMEM],
        out_specs=(VMEM,) * GROUPS,
        scratch_shapes=[pltpu.VMEM((BLOCK, BLOCK), F32)],
        compiler_params=PARAMS,
        name="second_left",
    )(group, received.reshape(SLABS, 2, HALF_TERMS * SLAB, BLOCK), left_env)


def live_only(value, first_row, live):
    rows = lax.broadcasted_iota(jnp.int32, value.shape, 0) + first_row
    cols = lax.broadcasted_iota(jnp.int32, value.shape, 1)
    return jnp.where((rows < live) & (cols < live), value, 0.0)


def second_carry_kernel(group_ref, dims_ref, right_ref, own_ref, *refs):
    *part_refs, out_ref, first_hbm, total, sem = refs
    value = own_ref[...]
    for part_ref in part_refs:
        value += part_ref[...].astype(F32)
    value = live_only(value, 0, dims_ref[0])
    total[...] = value
    first_row = pl.multiple_of(group_ref[0] * SHARE, SHARE)
    copy = pltpu.make_async_copy(total.at[pl.ds(first_row, SHARE), :], first_hbm.at[0], sem)
    copy.start()
    mean = jnp.sum(value * value, keepdims=True) * (1.0 / (SECTORS * BLOCK * BLOCK))
    high = mean.astype(BF16)
    rest = jnp.where(mean < jnp.inf, mean - high.astype(F32), 0.0)
    middle = rest.astype(BF16)
    low = (rest - middle.astype(F32)).astype(BF16)
    lane = lax.broadcasted_iota(jnp.int32, (SIDE_ROWS, LANES), 1)
    row = lax.broadcasted_iota(jnp.int32, (SIDE_ROWS, LANES), 0)
    pieces = jnp.where(lane == 0, high.astype(F32), 0.0)
    pieces = jnp.where(lane == 1, middle.astype(F32), pieces)
    pieces = jnp.where(lane == 2, low.astype(F32), pieces)
    pieces = jnp.where(row == 0, pieces, 0.0).astype(BF16)
    for slab in range(SLABS):
        for half in range(2):
            out_ref[slab, half, DATA_ROWS:, :] = pieces
    lifted = value * LIFT
    upper = lifted.astype(BF16)
    lower = (lifted - upper.astype(F32)).astype(BF16)
    for term in range(TERMS):
        right = right_ref[0, term]
        carried = jnp.dot(upper, right, preferred_element_type=F32)
        carried += jnp.dot(lower, right, preferred_element_type=F32)
        store_carried(term, carried, out_ref)
    copy.wait()


def second_carry(group, dims, right, own, parts):
    return pl.pallas_call(
        second_carry_kernel,
        out_shape=(
            jax.ShapeDtypeStruct((SLABS, 2, DATA_ROWS + SIDE_ROWS, LANES), BF16),
            jax.ShapeDtypeStruct((1, SHARE, BLOCK), F32),
        ),
        in_specs=[SMEM, SMEM] + [VMEM] * (GROUPS + 1),
        out_specs=(VMEM, HBM),
        scratch_shapes=[pltpu.VMEM((BLOCK, BLOCK), F32), pltpu.SemaphoreType.DMA],
        compiler_params=PARAMS,
        name="second_carry",
    )(group, dims, right, own, *parts)


def second_sum_kernel(group_ref, dims_ref, *refs):
    *part_refs, out_ref = refs
    value = (part_refs[0][...] + part_refs[1][...]) + (part_refs[2][...] + part_refs[3][...])
    out_ref[0] = live_only(value, group_ref[0] * SHARE, dims_ref[0])


def second_sum(group, dims, parts):
    return pl.pallas_call(
        second_sum_kernel,
        out_shape=jax.ShapeDtypeStruct((1, SHARE, BLOCK), F32),
        in_specs=[SMEM, SMEM] + [VMEM] * GROUPS,
        out_specs=VMEM,
        compiler_params=PARAMS,
        name="second_sum",
    )(group, dims, *parts)


def exchange(messages):
    messages = messages.reshape((SECTORS,) + messages.shape[-2:])
    return lax.all_to_all(messages, "sec", split_axis=0, concat_axis=0, tiled=True)


def shift(value, step):
    pairs = [(group, (group + step) % GROUPS) for group in range(GROUPS)]
    return lax.ppermute(value, "mpo", pairs)


def body(wavefunction, block_dims, left_env, right_env, task_left, task_term):
    group = lax.axis_index("mpo").astype(jnp.int32).reshape(1)
    carried = first_carry(block_dims, group, wavefunction, right_env, task_left, task_term)
    mixed, weights = first_mix(exchange(carried))
    own, sent = first_left(exchange(mixed), left_env)
    parts = [shift(sent, step) for step in range(1, GROUPS)]
    carried, first_product = second_carry(group, block_dims, right_env, own, parts)
    mixed = second_mix(exchange(carried), weights)
    parts = second_left(group, exchange(mixed), left_env)
    parts = [parts[0]] + [shift(parts[step], step) for step in range(1, GROUPS)]
    second_product = second_sum(group, block_dims, parts)
    return (first_product, second_product)


def solution(mesh):
    in_specs = (
        P("sec", None, None),
        P("sec"),
        P("sec", "mpo", None, None),
        P("sec", "mpo", None, None),
        P("sec", "mpo"),
        P("sec", "mpo"),
    )
    out_specs = (P("sec", "mpo", None), P("sec", "mpo", None))
    return jax.shard_map(body, mesh=mesh, in_specs=in_specs, out_specs=out_specs, check_vma=False)
```

time: 117 us -> 111 us (0.949)
  blocking collectives: 60.3 us -> 78.8 us
  waiting for transfers between devices: 25.6 us -> 11.7 us
  starting transfers between devices: 18 us -> 8.67 us
    all_to_all x3 -> x4, blocking collectives: 60.3 us -> 78.8 us  [exchange(): lax.all_to_all(messages, 'sec', split_axis=0, concat_axis=0, tiled=True)]
    all_to_all x1 -> x0, waiting for transfers between devices: 14.6 us -> none  [exchange(): lax.all_to_all(messages, 'sec', split_axis=0, concat_axis=0, tiled=True)]
    ppermute x9 -> x6, starting transfers between devices: 14 us -> 8.67 us  [shift(): return lax.ppermute(value, 'mpo', pairs)]
    all_to_all x1 -> x0, starting transfers between devices: 4.04 us -> none  [exchange(): lax.all_to_all(messages, 'sec', split_axis=0, concat_axis=0, tiled=True)]
    pallas_call x1, Pallas kernels: 0.37 us -> 2.61 us  [first_carry(): pl.pallas_call(first_carry_kernel, out_shape=jax.ShapeDtypeStruct((SLABS,...]
    pallas_call x1, Pallas kernels: 3.35 us -> 1.51 us  [first_mix(): pl.pallas_call(first_mix_kernel, out_shape=(jax.ShapeDtypeStruct((SECTORS...]
    unnamed x16 -> x12, local copies, waits for them, and re-layouts: 4.52 us -> 3.35 us
    ppermute x9 -> x6, waiting for transfers between devices: 11 us -> 11.7 us  [shift(): return lax.ppermute(value, 'mpo', pairs)]
  transfers between devices with their start and end apart: 10 -> 6, of which waited for: 8 -> 5; matrix products, arithmetic and copies ran while one was open for 0% -> 0% of each run, Pallas kernels for 0% -> 0%
where the time goes in v2:
time: 111 us
  blocking collectives  78.8 us (71%)
  waiting for transfers between devices  11.7 us (11%)
  starting transfers between devices  8.67 us (8%)
  Pallas kernels  6.95 us (6%)
  local copies, waits for them, and re-layouts  3.35 us (3%)
  between operations  1.36 us (1%)
    all_to_all x4, blocking collectives, exchange(): lax.all_to_all(messages, 'sec', split_axis=0, concat_axis=0, tiled=True)  78.8 us
    ppermute x6, waiting for transfers between devices, shift(): return lax.ppermute(value, 'mpo', pairs)  11.7 us
    ppermute x6, starting transfers between devices, shift(): return lax.ppermute(value, 'mpo', pairs)  8.67 us
    unnamed x12, local copies, waits for them, and re-layouts  3.35 us
    pallas_call x1, Pallas kernels, first_carry(): pl.pallas_call(first_carry_kernel, out_shape=jax.ShapeDtypeStruct((SLABS,...  2.61 us
  transfers between devices with their start and end apart: 6, of which 5 were waited for; matrix products, arithmetic and copies ran while one was open for 0% of the time, Pallas kernels for 0%

profile of v2, /device:TPU:0, one launch (start us, length us, event | category | flops | bytes accessed | tf_op | source)
XLA Modules:
  0.0 110.9 jit_solution(5515095898754627860)
XLA Ops:
  1.3 1.1 %copy-done = bf16[1,6,256,256]{3,2,1,0:T(8,128)(2,1)S(1)} copy-done((bf16[1,6,256,256]{3,2,1,0:T(8,128)(2,1)S(1)}, bf16[1,6,256,256]{3,2,1,0:T(8,128)(2,1)}, u32[]{:S(2)}) %copy-start) | copy-done | bytes 786456
  2.4 0.9 copy-done.3
  3.3 0.7 copy-done.4
  4.0 0.7 copy-done.5
  4.6 2.6 %first_carry.1 = bf16[16,2,112,128]{3,2,1,0:T(8,128)(2,1)S(1)} custom-call(s32[1]{0:T(128)S(6)} %copy.8.dims_ref, s32[1]{0:T(128)} %bitcast.group_ref, bf16[1,256,256]{2,1,0:T(8,128)(2,1)S(1)} %copy-done.3, bf16[1,6,256,256]{3,2,1,0:T(8,128)(2,1)S(1)} %copy-done, s32[1,32]{1,0:T(1,128)S(1)} %copy-done.4, s32[1,32]{1,0:T(1,128)S(1)} %copy-done.5), custom_call_target="tpu_custom_call" | custom-call | tf_op jit(solution)/shard_map/first_carry/pallas_call | solution.py:80
  7.3 23.1 %all_to_all.20.in_ref = bf16[32,112,128]{2,1,0:T(8,128)(2,1)S(1)} all-to-all(bf16[32,112,128]{2,1,0:T(8,128)(2,1)S(1)} %bitcast.5), channel_id=1, replica_groups=mesh['sec'=32,'mpo'=4] {'sec'}, dimensions={0} | all-to-all | bytes 1835008 | tf_op jit(solution)/shard_map/all_to_all | solution.py:299
  30.4 1.5 %first_mix.1 = (bf16[32,48,256]{2,1,0:T(8,128)(2,1)S(1)}, bf16[3,512,512]{2,1,0:T(8,128)(2,1)S(1)}) custom-call(bf16[32,112,128]{2,1,0:T(8,128)(2,1)S(1)} %all_to_all.20.in_ref), custom_call_target="tpu_custom_call" | custom-call | tf_op jit(solution)/shard_map/first_mix/pallas_call | solution.py:142
  31.9 18.1 %all_to_all.21 = bf16[32,48,256]{2,1,0:T(8,128)(2,1)S(1)} all-to-all(bf16[32,48,256]{2,1,0:T(8,128)(2,1)S(1)} %get-tuple-element.12), channel_id=1, replica_groups=mesh['sec'=32,'mpo'=4] {'sec'}, dimensions={0} | all-to-all | bytes 1572864 | tf_op jit(solution)/shard_map/all_to_all | solution.py:299
  50.0 0.4 first_left.1
  50.3 4.1 %collective-permute-start.2 = (bf16[256,256]{1,0:T(8,128)(2,1)S(1)}, bf16[256,256]{1,0:T(8,128)(2,1)S(1)}, u32[]{:S(2)}, u32[]{:S(2)}) collective-permute-start(bf16[256,256]{1,0:T(8,128)(2,1)S(1)} %get-tuple-element.14), channel_id=1, source_target_pairs={{0,3},{1,0},{2,1},{3,2},{4,7},{5,4},{6,5},{7,6},{8,11},{9,8},{10,9... | collective-permute-start | bytes 393224 | tf_op jit(solution)/shard_map/ppermute | solution.py:304
  54.5 1.3 %collective-permute-start = (bf16[256,256]{1,0:T(8,128)(2,1)S(1)}, bf16[256,256]{1,0:T(8,128)(2,1)S(1)}, u32[]{:S(2)}, u32[]{:S(2)}) collective-permute-start(bf16[256,256]{1,0:T(8,128)(2,1)S(1)} %get-tuple-element.14), channel_id=1, source_target_pairs={{0,1},{1,2},{2,3},{3,0},{4,5},{5,6},{6,7},{7,4},{8,9},{9,10},{10,1... | collective-permute-start | bytes 393224 | tf_op jit(solution)/shard_map/ppermute | solution.py:304
  55.7 4.4 %collective-permute-done.2.refs_2_ = bf16[256,256]{1,0:T(8,128)(2,1)S(1)} collective-permute-done((bf16[256,256]{1,0:T(8,128)(2,1)S(1)}, bf16[256,256]{1,0:T(8,128)(2,1)S(1)}, u32[]{:S(2)}, u32[]{:S(2)}) %collective-permute-start.2) | collective-permute-done | bytes 131104 | tf_op jit(solution)/shard_map/ppermute | solution.py:304
  60.1 2.2 %collective-permute-done.1.refs_1_ = bf16[256,256]{1,0:T(8,128)(2,1)S(1)} collective-permute-done((bf16[256,256]{1,0:T(8,128)(2,1)S(1)}, bf16[256,256]{1,0:T(8,128)(2,1)S(1)}, u32[]{:S(2)}, u32[]{:S(2)}) %collective-permute-start.1) | collective-permute-done | bytes 131104 | tf_op jit(solution)/shard_map/ppermute | solution.py:304
  62.4 1.2 %collective-permute-done.refs_0_ = bf16[256,256]{1,0:T(8,128)(2,1)S(1)} collective-permute-done((bf16[256,256]{1,0:T(8,128)(2,1)S(1)}, bf16[256,256]{1,0:T(8,128)(2,1)S(1)}, u32[]{:S(2)}, u32[]{:S(2)}) %collective-permute-start) | collective-permute-done | bytes 131104 | tf_op jit(solution)/shard_map/ppermute | solution.py:304
  63.5 0.8 second_carry.1
  64.4 19.7 %all_to_all.22.in_ref = bf16[32,112,128]{2,1,0:T(8,128)(2,1)S(1)} all-to-all(bf16[32,112,128]{2,1,0:T(8,128)(2,1)S(1)} %bitcast.8), channel_id=1, replica_groups=mesh['sec'=32,'mpo'=4] {'sec'}, dimensions={0} | all-to-all | bytes 1835008 | tf_op jit(solution)/shard_map/all_to_all | solution.py:299
  84.1 0.6 second_mix.1
  84.7 17.9 %all_to_all.23 = bf16[32,48,256]{2,1,0:T(8,128)(2,1)S(1)} all-to-all(bf16[32,48,256]{2,1,0:T(8,128)(2,1)S(1)} %second_mix.1), channel_id=1, replica_groups=mesh['sec'=32,'mpo'=4] {'sec'}, dimensions={0} | all-to-all | bytes 1572864 | tf_op jit(solution)/shard_map/all_to_all | solution.py:299
  102.6 0.4 second_left.1
  103.1 2.3 %collective-permute-start.4 = (f32[64,256]{1,0:T(8,128)S(1)}, f32[64,256]{1,0:T(8,128)S(1)}, u32[]{:S(2)}, u32[]{:S(2)}) collective-permute-start(f32[64,256]{1,0:T(8,128)S(1)} %get-tuple-element.20), channel_id=1, source_target_pairs={{0,2},{1,3},{2,0},{3,1},{4,6},{5,7},{6,4},{7,5},{8,10},{9,11},{10,... | collective-permute-start | bytes 196616 | tf_op jit(solution)/shard_map/ppermute | solution.py:304
  105.4 0.9 collective-permute-start.5
  106.3 3.3 %collective-permute-done.3.refs_1_ = f32[64,256]{1,0:T(8,128)S(1)} collective-permute-done((f32[64,256]{1,0:T(8,128)S(1)}, f32[64,256]{1,0:T(8,128)S(1)}, u32[]{:S(2)}, u32[]{:S(2)}) %collective-permute-start.3) | collective-permute-done | bytes 65568 | tf_op jit(solution)/shard_map/ppermute | solution.py:304
  109.6 0.6 collective-permute-done.5.refs_3_
  110.2 0.6 second_sum.1
  (11 shorter events, 0.1 us)
Async XLA Ops:
  1.3 1.1 %copy-start = (bf16[1,6,256,256]{3,2,1,0:T(8,128)(2,1)S(1)}, bf16[1,6,256,256]{3,2,1,0:T(8,128)(2,1)}, u32[]{:S(2)}) copy-start(bf16[1,6,256,256]{3,2,1,0:T(8,128)(2,1)} %right_ref.1) | copy-start | bytes 2359300
  2.4 0.9 copy-start.3
  3.3 0.7 copy-start.4
  4.0 0.7 copy-start.5
  30.4 19.6 %copy-start.2 = (bf16[1,6,256,256]{3,2,1,0:T(8,128)(2,1)S(1)}, bf16[1,6,256,256]{3,2,1,0:T(8,128)(2,1)}, u32[]{:S(2)}) copy-start(bf16[1,6,256,256]{3,2,1,0:T(8,128)(2,1)} %left_ref.3) | copy-start | bytes 2359300
  31.9 31.6 %copy-start.1 = (bf16[1,6,256,256]{3,2,1,0:T(8,128)(2,1)S(1)}, bf16[1,6,256,256]{3,2,1,0:T(8,128)(2,1)}, u32[]{:S(2)}) copy-start(bf16[1,6,256,256]{3,2,1,0:T(8,128)(2,1)} %right_ref.1) | copy-start | bytes 2359300
  50.3 9.8 %collective-permute-start.2 = (bf16[256,256]{1,0:T(8,128)(2,1)S(1)}, bf16[256,256]{1,0:T(8,128)(2,1)S(1)}, u32[]{:S(2)}, u32[]{:S(2)}) collective-permute-start(bf16[256,256]{1,0:T(8,128)(2,1)S(1)} %get-tuple-element.14), channel_id=1, source_target_pairs={{0,3},{1,0},{2,1},{3,2},{4,7},{5,4},{6,5},{7,6},{8,11},{9,8},{10,9... | collective-permute-start | bytes 393224 | tf_op jit(solution)/shard_map/ppermute | solution.py:304
  54.5 7.9 %collective-permute-start.1 = (bf16[256,256]{1,0:T(8,128)(2,1)S(1)}, bf16[256,256]{1,0:T(8,128)(2,1)S(1)}, u32[]{:S(2)}, u32[]{:S(2)}) collective-permute-start(bf16[256,256]{1,0:T(8,128)(2,1)S(1)} %get-tuple-element.14), channel_id=1, source_target_pairs={{0,2},{1,3},{2,0},{3,1},{4,6},{5,7},{6,4},{7,5},{8,10},{9,11},{10,... | collective-permute-start | bytes 393224 | tf_op jit(solution)/shard_map/ppermute | solution.py:304
  54.5 9.1 %collective-permute-start = (bf16[256,256]{1,0:T(8,128)(2,1)S(1)}, bf16[256,256]{1,0:T(8,128)(2,1)S(1)}, u32[]{:S(2)}, u32[]{:S(2)}) collective-permute-start(bf16[256,256]{1,0:T(8,128)(2,1)S(1)} %get-tuple-element.14), channel_id=1, source_target_pairs={{0,1},{1,2},{2,3},{3,0},{4,5},{5,6},{6,7},{7,4},{8,9},{9,10},{10,1... | collective-permute-start | bytes 393224 | tf_op jit(solution)/shard_map/ppermute | solution.py:304
  103.0 6.6 %collective-permute-start.3 = (f32[64,256]{1,0:T(8,128)S(1)}, f32[64,256]{1,0:T(8,128)S(1)}, u32[]{:S(2)}, u32[]{:S(2)}) collective-permute-start(f32[64,256]{1,0:T(8,128)S(1)} %get-tuple-element.19), channel_id=1, source_target_pairs={{0,1},{1,2},{2,3},{3,0},{4,5},{5,6},{6,7},{7,4},{8,9},{9,10},{10,1... | collective-permute-start | bytes 196616 | tf_op jit(solution)/shard_map/ppermute | solution.py:304
  103.1 6.5 %collective-permute-start.4 = (f32[64,256]{1,0:T(8,128)S(1)}, f32[64,256]{1,0:T(8,128)S(1)}, u32[]{:S(2)}, u32[]{:S(2)}) collective-permute-start(f32[64,256]{1,0:T(8,128)S(1)} %get-tuple-element.20), channel_id=1, source_target_pairs={{0,2},{1,3},{2,0},{3,1},{4,6},{5,7},{6,4},{7,5},{8,10},{9,11},{10,... | collective-permute-start | bytes 196616 | tf_op jit(solution)/shard_map/ppermute | solution.py:304
  105.4 4.8 %collective-permute-start.5 = (f32[64,256]{1,0:T(8,128)S(1)}, f32[64,256]{1,0:T(8,128)S(1)}, u32[]{:S(2)}, u32[]{:S(2)}) collective-permute-start(f32[64,256]{1,0:T(8,128)S(1)} %get-tuple-element.21), channel_id=1, source_target_pairs={{0,3},{1,0},{2,1},{3,2},{4,7},{5,4},{6,5},{7,6},{8,11},{9,8},{10,9... | collective-permute-start | bytes 196616 | tf_op jit(solution)/shard_map/ppermute | solution.py:304

commit v3 on v2

--- a/solution.py
+++ b/solution.py
@@ -16,7 +16,7 @@
 SHARE = BLOCK // GROUPS
 LANES = 128
 DATA_ROWS = HALF_TERMS * 2 * SLAB
-SIDE_ROWS = 16
+SIDE_ROWS = 8
 MIX = SECTORS * SLAB
 EPSILON = 1e-06
 LIFT = 512.0
@@ -76,7 +76,8 @@
         store_carried(term, carried, out_ref)
 
 
-def first_carry(dims, group, vector, right, left, term):
+def first_carry(dims, group, *fetched):
+    fetched = [pltpu.with_memory_space_constraint(array, pltpu.HBM) for array in fetched]
     return pl.pallas_call(
         first_carry_kernel,
         out_shape=jax.ShapeDtypeStruct((SLABS, 2, DATA_ROWS + SIDE_ROWS, LANES), BF16),
@@ -91,7 +92,7 @@
         ],
         compiler_params=PARAMS,
         name="first_carry",
-    )(dims, group, vector, right, left, term)
+    )(dims, group, *fetched)
 
 
 def mix_with(weights_ref, in_ref, out_ref, scale):
@@ -205,14 +206,16 @@
     total[...] = left_product(in_ref, left_ref)
     for step in range(GROUPS):
         owner = lax.rem(group_ref[0] + step, GROUPS)
-        out_refs[step][...] = total[pl.ds(pl.multiple_of(owner * SHARE, SHARE), SHARE), :]
+        part = total[pl.ds(pl.multiple_of(owner * SHARE, SHARE), SHARE), :]
+        out_refs[step][...] = part.astype(out_refs[step].dtype)
 
 
 def second_left(group, received, left_env):
-    share = jax.ShapeDtypeStruct((SHARE, BLOCK), F32)
+    own = jax.ShapeDtypeStruct((SHARE, BLOCK), F32)
+    sent = jax.ShapeDtypeStruct((SHARE, BLOCK), BF16)
     return pl.pallas_call(
         second_left_kernel,
-        out_shape=(share,) * GROUPS,
+        out_shape=(own,) + (sent,) * (GROUPS - 1),
         in_specs=[SMEM, VMEM, VMEM],
         out_specs=(VMEM,) * GROUPS,
         scratch_shapes=[pltpu.VMEM((BLOCK, BLOCK), F32)],
@@ -279,7 +282,9 @@
 
 def second_sum_kernel(group_ref, dims_ref, *refs):
     *part_refs, out_ref = refs
-    value = (part_refs[0][...] + part_refs[1][...]) + (part_refs[2][...] + part_refs[3][...])
+    value = part_refs[0][...]
+    for part_ref in part_refs[1:]:
+        value += part_ref[...].astype(F32)
     out_ref[0] = live_only(value, group_ref[0] * SHARE, dims_ref[0])
 
 

time: 111 us -> 105 us (0.946)
  local copies, waits for them, and re-layouts: 3.35 us -> 0.01 us
  blocking collectives: 78.8 us -> 77.4 us
    unnamed x12 -> x4, local copies, waits for them, and re-layouts: 3.35 us -> 0.01 us
    all_to_all x4, blocking collectives: 78.8 us -> 77.4 us  [exchange(): lax.all_to_all(messages, 'sec', split_axis=0, concat_axis=0, tiled=True)]
  transfers between devices with their start and end apart: 6 -> 6, of which waited for: 5 -> 6; matrix products, arithmetic and copies ran while one was open for 0% -> 0% of each run, Pallas kernels for 0% -> 0%
where the time goes in v3:
time: 105 us
  blocking collectives  77.4 us (74%)
  waiting for transfers between devices  10.9 us (10%)
  starting transfers between devices  8.67 us (8%)
  Pallas kernels  6.72 us (6%)
  between operations  1.35 us (1%)
    all_to_all x4, blocking collectives, exchange(): lax.all_to_all(messages, 'sec', split_axis=0, concat_axis=0, tiled=True)  77.4 us
    ppermute x6, waiting for transfers between devices, shift(): return lax.ppermute(value, 'mpo', pairs)  10.9 us
    ppermute x6, starting transfers between devices, shift(): return lax.ppermute(value, 'mpo', pairs)  8.67 us
    pallas_call x1, Pallas kernels, first_carry(): pl.pallas_call(first_carry_kernel, out_shape=jax.ShapeDtypeStruct((SLABS,...  2.38 us
  transfers between devices with their start and end apart: 6, of which 6 were waited for; matrix products, arithmetic and copies ran while one was open for 0% of the time, Pallas kernels for 0%

profile of v3, /device:TPU:0, one launch (start us, length us, event | category | flops | bytes accessed | tf_op | source)
XLA Modules:
  0.0 105.1 jit_solution(14554280391153773816)
XLA Ops:
  1.3 2.4 %first_carry.1 = bf16[16,2,104,128]{3,2,1,0:T(8,128)(2,1)S(1)} custom-call(s32[1]{0:T(128)S(6)} %copy.8.dims_ref, s32[1]{0:T(128)} %bitcast.group_ref, bf16[1,256,256]{2,1,0:T(8,128)(2,1)} %vector_hbm.1, bf16[1,6,256,256]{3,2,1,0:T(8,128)(2,1)} %right_ref.1, s32[1,32]{1,0:T(1,128)} %left_hbm.1, s32[1,32]{1,0:T(1,128)} %term_hbm.1), custom_call_target="tpu_custom_call" | custom-call | tf_op jit(solution)/shard_map/first_carry/pallas_call | solution.py:81
  3.7 22.4 %all_to_all.20.in_ref = bf16[32,104,128]{2,1,0:T(8,128)(2,1)S(1)} all-to-all(bf16[32,104,128]{2,1,0:T(8,128)(2,1)S(1)} %bitcast.5), channel_id=1, replica_groups=mesh['sec'=32,'mpo'=4] {'sec'}, dimensions={0} | all-to-all | bytes 1703936 | tf_op jit(solution)/shard_map/all_to_all | solution.py:304
  26.1 1.5 %first_mix.1 = (bf16[32,48,256]{2,1,0:T(8,128)(2,1)S(1)}, bf16[3,512,512]{2,1,0:T(8,128)(2,1)S(1)}) custom-call(bf16[32,104,128]{2,1,0:T(8,128)(2,1)S(1)} %all_to_all.20.in_ref), custom_call_target="tpu_custom_call" | custom-call | tf_op jit(solution)/shard_map/first_mix/pallas_call | solution.py:143
  27.6 0.0 copy-start
  27.6 18.1 %all_to_all.21 = bf16[32,48,256]{2,1,0:T(8,128)(2,1)S(1)} all-to-all(bf16[32,48,256]{2,1,0:T(8,128)(2,1)S(1)} %get-tuple-element.12), channel_id=1, replica_groups=mesh['sec'=32,'mpo'=4] {'sec'}, dimensions={0} | all-to-all | bytes 1572864 | tf_op jit(solution)/shard_map/all_to_all | solution.py:304
  45.7 0.4 first_left.1
  46.1 4.1 %collective-permute-start.2 = (bf16[256,256]{1,0:T(8,128)(2,1)S(1)}, bf16[256,256]{1,0:T(8,128)(2,1)S(1)}, u32[]{:S(2)}, u32[]{:S(2)}) collective-permute-start(bf16[256,256]{1,0:T(8,128)(2,1)S(1)} %get-tuple-element.14), channel_id=1, source_target_pairs={{0,3},{1,0},{2,1},{3,2},{4,7},{5,4},{6,5},{7,6},{8,11},{9,8},{10,9... | collective-permute-start | bytes 393224 | tf_op jit(solution)/shard_map/ppermute | solution.py:309
  50.2 0.0 collective-permute-start.1
  50.2 1.3 %collective-permute-start = (bf16[256,256]{1,0:T(8,128)(2,1)S(1)}, bf16[256,256]{1,0:T(8,128)(2,1)S(1)}, u32[]{:S(2)}, u32[]{:S(2)}) collective-permute-start(bf16[256,256]{1,0:T(8,128)(2,1)S(1)} %get-tuple-element.14), channel_id=1, source_target_pairs={{0,1},{1,2},{2,3},{3,0},{4,5},{5,6},{6,7},{7,4},{8,9},{9,10},{10,1... | collective-permute-start | bytes 393224 | tf_op jit(solution)/shard_map/ppermute | solution.py:309
  51.4 4.4 %collective-permute-done.2.refs_2_ = bf16[256,256]{1,0:T(8,128)(2,1)S(1)} collective-permute-done((bf16[256,256]{1,0:T(8,128)(2,1)S(1)}, bf16[256,256]{1,0:T(8,128)(2,1)S(1)}, u32[]{:S(2)}, u32[]{:S(2)}) %collective-permute-start.2) | collective-permute-done | bytes 131104 | tf_op jit(solution)/shard_map/ppermute | solution.py:309
  55.8 2.2 %collective-permute-done.1.refs_1_ = bf16[256,256]{1,0:T(8,128)(2,1)S(1)} collective-permute-done((bf16[256,256]{1,0:T(8,128)(2,1)S(1)}, bf16[256,256]{1,0:T(8,128)(2,1)S(1)}, u32[]{:S(2)}, u32[]{:S(2)}) %collective-permute-start.1) | collective-permute-done | bytes 131104 | tf_op jit(solution)/shard_map/ppermute | solution.py:309
  58.1 1.2 %collective-permute-done.refs_0_ = bf16[256,256]{1,0:T(8,128)(2,1)S(1)} collective-permute-done((bf16[256,256]{1,0:T(8,128)(2,1)S(1)}, bf16[256,256]{1,0:T(8,128)(2,1)S(1)}, u32[]{:S(2)}, u32[]{:S(2)}) %collective-permute-start) | collective-permute-done | bytes 131104 | tf_op jit(solution)/shard_map/ppermute | solution.py:309
  59.3 0.8 second_carry.1
  60.1 19.0 %all_to_all.22.in_ref = bf16[32,104,128]{2,1,0:T(8,128)(2,1)S(1)} all-to-all(bf16[32,104,128]{2,1,0:T(8,128)(2,1)S(1)} %bitcast.8), channel_id=1, replica_groups=mesh['sec'=32,'mpo'=4] {'sec'}, dimensions={0} | all-to-all | bytes 1703936 | tf_op jit(solution)/shard_map/all_to_all | solution.py:304
  79.1 0.6 second_mix.1
  79.7 17.9 %all_to_all.23 = bf16[32,48,256]{2,1,0:T(8,128)(2,1)S(1)} all-to-all(bf16[32,48,256]{2,1,0:T(8,128)(2,1)S(1)} %second_mix.1), channel_id=1, replica_groups=mesh['sec'=32,'mpo'=4] {'sec'}, dimensions={0} | all-to-all | bytes 1572864 | tf_op jit(solution)/shard_map/all_to_all | solution.py:304
  97.6 0.4 second_left.1
  98.0 0.1 collective-permute-start.3
  98.1 2.3 %collective-permute-start.4 = (bf16[64,256]{1,0:T(8,128)(2,1)S(1)}, bf16[64,256]{1,0:T(8,128)(2,1)S(1)}, u32[]{:S(2)}, u32[]{:S(2)}) collective-permute-start(bf16[64,256]{1,0:T(8,128)(2,1)S(1)} %get-tuple-element.20), channel_id=1, source_target_pairs={{0,2},{1,3},{2,0},{3,1},{4,6},{5,7},{6,4},{7,5},{8,10},{9,11},{10,... | collective-permute-start | bytes 98312 | tf_op jit(solution)/shard_map/ppermute | solution.py:309
  100.4 0.9 collective-permute-start.5
  101.3 1.9 %collective-permute-done.3.refs_1_ = bf16[64,256]{1,0:T(8,128)(2,1)S(1)} collective-permute-done((bf16[64,256]{1,0:T(8,128)(2,1)S(1)}, bf16[64,256]{1,0:T(8,128)(2,1)S(1)}, u32[]{:S(2)}, u32[]{:S(2)}) %collective-permute-start.3) | collective-permute-done | bytes 32800 | tf_op jit(solution)/shard_map/ppermute | solution.py:309
  103.2 0.4 collective-permute-done.4.refs_2_
  103.6 0.8 collective-permute-done.5.refs_3_
  104.4 0.7 second_sum.1
  (3 shorter events, 0.0 us)
Async XLA Ops:
  26.1 19.6 %copy-start.1 = (bf16[1,6,256,256]{3,2,1,0:T(8,128)(2,1)S(1)}, bf16[1,6,256,256]{3,2,1,0:T(8,128)(2,1)}, u32[]{:S(2)}) copy-start(bf16[1,6,256,256]{3,2,1,0:T(8,128)(2,1)} %left_ref.3) | copy-start | bytes 2359300
  27.6 31.6 %copy-start = (bf16[1,6,256,256]{3,2,1,0:T(8,128)(2,1)S(1)}, bf16[1,6,256,256]{3,2,1,0:T(8,128)(2,1)}, u32[]{:S(2)}) copy-start(bf16[1,6,256,256]{3,2,1,0:T(8,128)(2,1)} %right_ref.1) | copy-start | bytes 2359300
  46.1 9.8 %collective-permute-start.2 = (bf16[256,256]{1,0:T(8,128)(2,1)S(1)}, bf16[256,256]{1,0:T(8,128)(2,1)S(1)}, u32[]{:S(2)}, u32[]{:S(2)}) collective-permute-start(bf16[256,256]{1,0:T(8,128)(2,1)S(1)} %get-tuple-element.14), channel_id=1, source_target_pairs={{0,3},{1,0},{2,1},{3,2},{4,7},{5,4},{6,5},{7,6},{8,11},{9,8},{10,9... | collective-permute-start | bytes 393224 | tf_op jit(solution)/shard_map/ppermute | solution.py:309
  50.2 7.9 %collective-permute-start.1 = (bf16[256,256]{1,0:T(8,128)(2,1)S(1)}, bf16[256,256]{1,0:T(8,128)(2,1)S(1)}, u32[]{:S(2)}, u32[]{:S(2)}) collective-permute-start(bf16[256,256]{1,0:T(8,128)(2,1)S(1)} %get-tuple-element.14), channel_id=1, source_target_pairs={{0,2},{1,3},{2,0},{3,1},{4,6},{5,7},{6,4},{7,5},{8,10},{9,11},{10,... | collective-permute-start | bytes 393224 | tf_op jit(solution)/shard_map/ppermute | solution.py:309
  50.2 9.1 %collective-permute-start = (bf16[256,256]{1,0:T(8,128)(2,1)S(1)}, bf16[256,256]{1,0:T(8,128)(2,1)S(1)}, u32[]{:S(2)}, u32[]{:S(2)}) collective-permute-start(bf16[256,256]{1,0:T(8,128)(2,1)S(1)} %get-tuple-element.14), channel_id=1, source_target_pairs={{0,1},{1,2},{2,3},{3,0},{4,5},{5,6},{6,7},{7,4},{8,9},{9,10},{10,1... | collective-permute-start | bytes 393224 | tf_op jit(solution)/shard_map/ppermute | solution.py:309
  98.0 5.2 %collective-permute-start.3 = (bf16[64,256]{1,0:T(8,128)(2,1)S(1)}, bf16[64,256]{1,0:T(8,128)(2,1)S(1)}, u32[]{:S(2)}, u32[]{:S(2)}) collective-permute-start(bf16[64,256]{1,0:T(8,128)(2,1)S(1)} %get-tuple-element.19), channel_id=1, source_target_pairs={{0,1},{1,2},{2,3},{3,0},{4,5},{5,6},{6,7},{7,4},{8,9},{9,10},{10,1... | collective-permute-start | bytes 98312 | tf_op jit(solution)/shard_map/ppermute | solution.py:309
  98.1 5.5 %collective-permute-start.4 = (bf16[64,256]{1,0:T(8,128)(2,1)S(1)}, bf16[64,256]{1,0:T(8,128)(2,1)S(1)}, u32[]{:S(2)}, u32[]{:S(2)}) collective-permute-start(bf16[64,256]{1,0:T(8,128)(2,1)S(1)} %get-tuple-element.20), channel_id=1, source_target_pairs={{0,2},{1,3},{2,0},{3,1},{4,6},{5,7},{6,4},{7,5},{8,10},{9,11},{10,... | collective-permute-start | bytes 98312 | tf_op jit(solution)/shard_map/ppermute | solution.py:309
  100.4 4.0 %collective-permute-start.5 = (bf16[64,256]{1,0:T(8,128)(2,1)S(1)}, bf16[64,256]{1,0:T(8,128)(2,1)S(1)}, u32[]{:S(2)}, u32[]{:S(2)}) collective-permute-start(bf16[64,256]{1,0:T(8,128)(2,1)S(1)} %get-tuple-element.21), channel_id=1, source_target_pairs={{0,3},{1,0},{2,1},{3,2},{4,7},{5,4},{6,5},{7,6},{8,11},{9,8},{10,9... | collective-permute-start | bytes 98312 | tf_op jit(solution)/shard_map/ppermute | solution.py:309

commit v4 on v3

--- a/solution.py
+++ b/solution.py
@@ -38,61 +38,66 @@
         out_ref[:, half, row : row + SLAB, :] = part
 
 
-def first_carry_kernel(
-    dims_ref, group_ref, vector_hbm, right_hbm, left_hbm, term_hbm, out_ref, vector_ref, right_ref, left_ref, term_ref, sems
-):
-    del group_ref
+def fetch_kernel(*refs):
+    from_refs, to_refs, sems = refs[:4], refs[4:8], refs[8]
     copies = [
-        pltpu.make_async_copy(left_hbm, left_ref, sems.at[TERMS]),
-        pltpu.make_async_copy(term_hbm, term_ref, sems.at[TERMS + 1]),
-        pltpu.make_async_copy(vector_hbm, vector_ref, sems.at[TERMS + 2]),
+        pltpu.make_async_copy(from_ref, to_ref, sems.at[index])
+        for index, (from_ref, to_ref) in enumerate(zip(from_refs, to_refs))
     ]
-    fetches = [
-        pltpu.make_async_copy(right_hbm.at[0, term], right_ref.at[0, term], sems.at[term])
-        for term in range(TERMS)
-    ]
-    for copy in copies + fetches:
+    for copy in copies:
         copy.start()
-    copies[0].wait()
-    copies[1].wait()
-    targets = left_ref[...]
-    terms = term_ref[...]
-    for half in range(2):
-        place = terms - half * HALF_TERMS
-        inside = (place >= 0) & (place < HALF_TERMS)
-        code = jnp.where(inside, targets + place * SECTORS, 255).astype(F32)
-        code = jnp.broadcast_to(code, (SIDE_ROWS, TASKS)).astype(BF16)
-        for slab in range(SLABS):
-            out_ref[slab, half, DATA_ROWS:, :] = jnp.zeros((SIDE_ROWS, LANES), BF16)
-            out_ref[slab, half, DATA_ROWS:, :TASKS] = code
-    copies[2].wait()
+    for copy in copies:
+        copy.wait()
+
+
+def fetch(*arrays):
+    arrays = [pltpu.with_memory_space_constraint(array, pltpu.HBM) for array in arrays]
+    return pl.pallas_call(
+        fetch_kernel,
+        out_shape=[jax.ShapeDtypeStruct(array.shape, array.dtype) for array in arrays],
+        in_specs=[HBM] * len(arrays),
+        out_specs=[VMEM] * len(arrays),
+        scratch_shapes=[pltpu.SemaphoreType.DMA((len(arrays),))],
+        compiler_params=PARAMS,
+        name="fetch",
+    )(*arrays)
+
+
+def first_carry_kernel(dims_ref, right_ref, vector_ref, left_ref, term_ref, out_ref, live_ref):
     live = dims_ref[0]
-    rows = lax.broadcasted_iota(jnp.int32, (BLOCK, BLOCK), 0)
-    cols = lax.broadcasted_iota(jnp.int32, (BLOCK, BLOCK), 1)
-    vector = jnp.where((rows < live) & (cols < live), vector_ref[0].astype(F32), 0.0).astype(BF16)
+    live_ref[...] = jnp.full((8, LANES), live, jnp.int32)
+    vector = live_only(vector_ref[0].astype(F32), 0, live).astype(BF16)
     for term in range(TERMS):
-        fetches[term].wait()
         carried = jnp.dot(vector, right_ref[0, term], preferred_element_type=F32)
         store_carried(term, carried, out_ref)
-
-
-def first_carry(dims, group, *fetched):
-    fetched = [pltpu.with_memory_space_constraint(array, pltpu.HBM) for array in fetched]
+    line = lax.broadcasted_iota(jnp.int32, (LANES, TASKS), 0)
+    for half in range(2):
+        place = term_ref[...] - half * HALF_TERMS
+        inside = (place >= 0) & (place < HALF_TERMS)
+        code = jnp.where(inside, left_ref[...] + place * SECTORS, -1)
+        named = jnp.where(line == code, 1.0, 0.0).astype(BF16)
+        count = lax.dot_general(
+            jnp.ones((SIDE_ROWS, TASKS), BF16),
+            named,
+            (((1,), (1,)), ((), ())),
+            preferred_element_type=F32,
+        ).astype(BF16)
+        for slab in range(SLABS):
+            out_ref[slab, half, DATA_ROWS:, :] = count
+
+
+def first_carry(dims, fetched):
     return pl.pallas_call(
         first_carry_kernel,
-        out_shape=jax.ShapeDtypeStruct((SLABS, 2, DATA_ROWS + SIDE_ROWS, LANES), BF16),
-        in_specs=[SMEM, SMEM, HBM, HBM, HBM, HBM],
-        out_specs=VMEM,
-        scratch_shapes=[
-            pltpu.VMEM((1, BLOCK, BLOCK), BF16),
-            pltpu.VMEM((1, TERMS, BLOCK, BLOCK), BF16),
-            pltpu.VMEM((1, TASKS), jnp.int32),
-            pltpu.VMEM((1, TASKS), jnp.int32),
-            pltpu.SemaphoreType.DMA((TERMS + 3,)),
-        ],
+        out_shape=(
+            jax.ShapeDtypeStruct((SLABS, 2, DATA_ROWS + SIDE_ROWS, LANES), BF16),
+            jax.ShapeDtypeStruct((8, LANES), jnp.int32),
+        ),
+        in_specs=[SMEM] + [VMEM] * 4,
+        out_specs=(VMEM, VMEM),
         compiler_params=PARAMS,
         name="first_carry",
-    )(dims, group, *fetched)
+    )(dims, *fetched)
 
 
 def mix_with(weights_ref, in_ref, out_ref, scale):
@@ -111,16 +116,10 @@
 
 
 def first_mix_kernel(in_ref, out_ref, weights_ref, wide_ref):
-    codes = in_ref[:, DATA_ROWS : DATA_ROWS + SIDE_ROWS, :].astype(F32)[:, 0, :]
-    lanes = lax.broadcasted_iota(jnp.int32, (SECTORS, LANES), 1).astype(F32)
-    counts = jnp.zeros((SECTORS, LANES), F32)
-    for task in range(TASKS):
-        counts += jnp.where(codes[:, task : task + 1] == lanes, 1.0, 0.0)
-    counts = counts.astype(BF16)
-    spread = (
-        lax.broadcasted_iota(jnp.int32, (SECTORS, MIX), 0)
-        == lax.broadcasted_iota(jnp.int32, (SECTORS, MIX), 1) // SLAB
-    )
+    counts = in_ref[:, DATA_ROWS:, :].reshape(SECTORS * SIDE_ROWS, LANES)
+    sent_row = lax.broadcasted_iota(jnp.int32, (SECTORS * SIDE_ROWS, MIX), 0)
+    mixed_row = lax.broadcasted_iota(jnp.int32, (SECTORS * SIDE_ROWS, MIX), 1)
+    spread = sent_row == mixed_row // SLAB * SIDE_ROWS
     spread = jnp.where(spread, 1.0, 0.0).astype(BF16)
     wide_ref[...] = lax.dot_general(
         counts, spread, (((0,), (0,)), ((), ())), preferred_element_type=F32
@@ -201,27 +200,28 @@
     )(received.reshape(SLABS, 2, HALF_TERMS * SLAB, BLOCK), left_env)
 
 
-def second_left_kernel(group_ref, in_ref, left_ref, *refs):
+def second_left_kernel(in_ref, left_ref, *refs):
     *out_refs, total = refs
+    group = lax.axis_index("mpo")
     total[...] = left_product(in_ref, left_ref)
     for step in range(GROUPS):
-        owner = lax.rem(group_ref[0] + step, GROUPS)
+        owner = lax.rem(group + step, GROUPS)
         part = total[pl.ds(pl.multiple_of(owner * SHARE, SHARE), SHARE), :]
         out_refs[step][...] = part.astype(out_refs[step].dtype)
 
 
-def second_left(group, received, left_env):
+def second_left(received, left_env):
     own = jax.ShapeDtypeStruct((SHARE, BLOCK), F32)
     sent = jax.ShapeDtypeStruct((SHARE, BLOCK), BF16)
     return pl.pallas_call(
         second_left_kernel,
         out_shape=(own,) + (sent,) * (GROUPS - 1),
-        in_specs=[SMEM, VMEM, VMEM],
+        in_specs=[VMEM, VMEM],
         out_specs=(VMEM,) * GROUPS,
         scratch_shapes=[pltpu.VMEM((BLOCK, BLOCK), F32)],
         compiler_params=PARAMS,
         name="second_left",
-    )(group, received.reshape(SLABS, 2, HALF_TERMS * SLAB, BLOCK), left_env)
+    )(received.reshape(SLABS, 2, HALF_TERMS * SLAB, BLOCK), left_env)
 
 
 def live_only(value, first_row, live):
@@ -230,14 +230,14 @@
     return jnp.where((rows < live) & (cols < live), value, 0.0)
 
 
-def second_carry_kernel(group_ref, dims_ref, right_ref, own_ref, *refs):
+def second_carry_kernel(live_ref, right_ref, own_ref, *refs):
     *part_refs, out_ref, first_hbm, total, sem = refs
     value = own_ref[...]
     for part_ref in part_refs:
         value += part_ref[...].astype(F32)
-    value = live_only(value, 0, dims_ref[0])
+    value = live_only(value, 0, live_ref[:1, :1])
     total[...] = value
-    first_row = pl.multiple_of(group_ref[0] * SHARE, SHARE)
+    first_row = pl.multiple_of(lax.axis_index("mpo") * SHARE, SHARE)
     copy = pltpu.make_async_copy(total.at[pl.ds(first_row, SHARE), :], first_hbm.at[0], sem)
     copy.start()
     mean = jnp.sum(value * value, keepdims=True) * (1.0 / (SECTORS * BLOCK * BLOCK))
@@ -257,46 +257,45 @@
     lifted = value * LIFT
     upper = lifted.astype(BF16)
     lower = (lifted - upper.astype(F32)).astype(BF16)
+    both = jnp.concatenate([upper, lower], axis=0)
     for term in range(TERMS):
-        right = right_ref[0, term]
-        carried = jnp.dot(upper, right, preferred_element_type=F32)
-        carried += jnp.dot(lower, right, preferred_element_type=F32)
-        store_carried(term, carried, out_ref)
+        carried = jnp.dot(both, right_ref[0, term], preferred_element_type=F32)
+        store_carried(term, carried[:BLOCK] + carried[BLOCK:], out_ref)
     copy.wait()
 
 
-def second_carry(group, dims, right, own, parts):
+def second_carry(live, right, own, parts):
     return pl.pallas_call(
         second_carry_kernel,
         out_shape=(
             jax.ShapeDtypeStruct((SLABS, 2, DATA_ROWS + SIDE_ROWS, LANES), BF16),
             jax.ShapeDtypeStruct((1, SHARE, BLOCK), F32),
         ),
-        in_specs=[SMEM, SMEM] + [VMEM] * (GROUPS + 1),
+        in_specs=[VMEM] * (GROUPS + 2),
         out_specs=(VMEM, HBM),
         scratch_shapes=[pltpu.VMEM((BLOCK, BLOCK), F32), pltpu.SemaphoreType.DMA],
         compiler_params=PARAMS,
         name="second_carry",
-    )(group, dims, right, own, *parts)
-
-
-def second_sum_kernel(group_ref, dims_ref, *refs):
+    )(live, right, own, *parts)
+
+
+def second_sum_kernel(live_ref, *refs):
     *part_refs, out_ref = refs
     value = part_refs[0][...]
     for part_ref in part_refs[1:]:
         value += part_ref[...].astype(F32)
-    out_ref[0] = live_only(value, group_ref[0] * SHARE, dims_ref[0])
-
-
-def second_sum(group, dims, parts):
+    out_ref[0] = live_only(value, lax.axis_index("mpo") * SHARE, live_ref[:1, :1])
+
+
+def second_sum(live, parts):
     return pl.pallas_call(
         second_sum_kernel,
         out_shape=jax.ShapeDtypeStruct((1, SHARE, BLOCK), F32),
-        in_specs=[SMEM, SMEM] + [VMEM] * GROUPS,
+        in_specs=[VMEM] * (GROUPS + 1),
         out_specs=VMEM,
         compiler_params=PARAMS,
         name="second_sum",
-    )(group, dims, *parts)
+    )(live, *parts)
 
 
 def exchange(messages):
@@ -310,16 +309,16 @@
 
 
 def body(wavefunction, block_dims, left_env, right_env, task_left, task_term):
-    group = lax.axis_index("mpo").astype(jnp.int32).reshape(1)
-    carried = first_carry(block_dims, group, wavefunction, right_env, task_left, task_term)
+    fetched = fetch(right_env, wavefunction, task_left, task_term)
+    carried, live = first_carry(block_dims, fetched)
     mixed, weights = first_mix(exchange(carried))
     own, sent = first_left(exchange(mixed), left_env)
-    parts = [shift(sent, step) for step in range(1, GROUPS)]
-    carried, first_product = second_carry(group, block_dims, right_env, own, parts)
+    parts = [shift(sent, step) for step in (2, 3, 1)]
+    carried, first_product = second_carry(live, fetched[0], own, parts)
     mixed = second_mix(exchange(carried), weights)
-    parts = second_left(group, exchange(mixed), left_env)
-    parts = [parts[0]] + [shift(parts[step], step) for step in range(1, GROUPS)]
-    second_product = second_sum(group, block_dims, parts)
+    parts = second_left(exchange(mixed), left_env)
+    parts = [parts[0]] + [shift(parts[step], step) for step in (2, 1, 3)]
+    second_product = second_sum(live, parts)
     return (first_product, second_product)
 
 

time: 105 us -> 102 us (0.971)
  waiting for transfers between devices: 10.9 us -> 8.45 us
  Pallas kernels: 6.72 us -> 5.16 us
  starting transfers between devices: 8.67 us -> 9.95 us
    ppermute x6, waiting for transfers between devices: 10.9 us -> 8.45 us  [shift(): return lax.ppermute(value, 'mpo', pairs)]
    ppermute x6, starting transfers between devices: 8.67 us -> 9.95 us  [shift(): return lax.ppermute(value, 'mpo', pairs)]
    pallas_call x1 -> x2, Pallas kernels: 2.38 us -> 1.56 us  [the longest x1 1.18 us: fetch(): pl.pallas_call(fetch_kernel, out_shape=[jax.ShapeDtypeStruct(array.shape,...]
where the time goes in v4:
time: 102 us
  blocking collectives  77.2 us (76%)
  starting transfers between devices  9.95 us (10%)
  waiting for transfers between devices  8.45 us (8%)
  Pallas kernels  5.16 us (5%)
  between operations  1.34 us (1%)
    all_to_all x4, blocking collectives, exchange(): lax.all_to_all(messages, 'sec', split_axis=0, concat_axis=0, tiled=True)  77.2 us
    ppermute x6, starting transfers between devices, shift(): return lax.ppermute(value, 'mpo', pairs)  9.95 us
    ppermute x6, waiting for transfers between devices, shift(): return lax.ppermute(value, 'mpo', pairs)  8.45 us
  transfers between devices with their start and end apart: 6, of which 6 were waited for; matrix products, arithmetic and copies ran while one was open for 0% of the time, Pallas kernels for 0%

profile of v4, /device:TPU:0, one launch (start us, length us, event | category | flops | bytes accessed | tf_op | source)
XLA Modules:
  0.0 102.1 jit_solution(12279733378692179632)
XLA Ops:
  1.3 1.2 %fetch.1 = (bf16[1,6,256,256]{3,2,1,0:T(8,128)(2,1)S(1)}, bf16[1,256,256]{2,1,0:T(8,128)(2,1)S(1)}, s32[1,32]{1,0:T(1,128)S(1)}, s32[1,32]{1,0:T(1,128)S(1)}) custom-call(bf16[1,6,256,256]{3,2,1,0:T(8,128)(2,1)} %refs_0_.1, bf16[1,256,256]{2,1,0:T(8,128)(2,1)} %refs_1_.1, s32[1,32]{1,0:T(1,128)} %refs_2_.1, s32[1,32]{1,0:T(1,128)} %refs_3_.1), custom_call_target="tpu_custom_call" | custom-call | tf_op jit(solution)/shard_map/fetch/pallas_call | solution.py:55
  2.5 0.4 first_carry.1
  2.9 22.4 %all_to_all.20.in_ref = bf16[32,104,128]{2,1,0:T(8,128)(2,1)S(1)} all-to-all(bf16[32,104,128]{2,1,0:T(8,128)(2,1)S(1)} %bitcast.7), channel_id=1, replica_groups=mesh['sec'=32,'mpo'=4] {'sec'}, dimensions={0} | all-to-all | bytes 1703936 | tf_op jit(solution)/shard_map/all_to_all | solution.py:303
  25.3 0.8 first_mix.1
  26.1 17.9 %all_to_all.21 = bf16[32,48,256]{2,1,0:T(8,128)(2,1)S(1)} all-to-all(bf16[32,48,256]{2,1,0:T(8,128)(2,1)S(1)} %get-tuple-element.24), channel_id=1, replica_groups=mesh['sec'=32,'mpo'=4] {'sec'}, dimensions={0} | all-to-all | bytes 1572864 | tf_op jit(solution)/shard_map/all_to_all | solution.py:303
  44.0 0.4 first_left.1
  44.4 2.0 %collective-permute-start.2 = (bf16[256,256]{1,0:T(8,128)(2,1)S(1)}, bf16[256,256]{1,0:T(8,128)(2,1)S(1)}, u32[]{:S(2)}, u32[]{:S(2)}) collective-permute-start(bf16[256,256]{1,0:T(8,128)(2,1)S(1)} %get-tuple-element.26), channel_id=1, source_target_pairs={{0,1},{1,2},{2,3},{3,0},{4,5},{5,6},{6,7},{7,4},{8,9},{9,10},{10,1... | collective-permute-start | bytes 393224 | tf_op jit(solution)/shard_map/ppermute | solution.py:308
  46.4 2.2 %collective-permute-start.1 = (bf16[256,256]{1,0:T(8,128)(2,1)S(1)}, bf16[256,256]{1,0:T(8,128)(2,1)S(1)}, u32[]{:S(2)}, u32[]{:S(2)}) collective-permute-start(bf16[256,256]{1,0:T(8,128)(2,1)S(1)} %get-tuple-element.26), channel_id=1, source_target_pairs={{0,3},{1,0},{2,1},{3,2},{4,7},{5,4},{6,5},{7,6},{8,11},{9,8},{10,9... | collective-permute-start | bytes 393224 | tf_op jit(solution)/shard_map/ppermute | solution.py:308
  48.6 1.8 %collective-permute-start = (bf16[256,256]{1,0:T(8,128)(2,1)S(1)}, bf16[256,256]{1,0:T(8,128)(2,1)S(1)}, u32[]{:S(2)}, u32[]{:S(2)}) collective-permute-start(bf16[256,256]{1,0:T(8,128)(2,1)S(1)} %get-tuple-element.26), channel_id=1, source_target_pairs={{0,2},{1,3},{2,0},{3,1},{4,6},{5,7},{6,4},{7,5},{8,10},{9,11},{10,... | collective-permute-start | bytes 393224 | tf_op jit(solution)/shard_map/ppermute | solution.py:308
  50.3 1.7 %collective-permute-done.2.refs_2_ = bf16[256,256]{1,0:T(8,128)(2,1)S(1)} collective-permute-done((bf16[256,256]{1,0:T(8,128)(2,1)S(1)}, bf16[256,256]{1,0:T(8,128)(2,1)S(1)}, u32[]{:S(2)}, u32[]{:S(2)}) %collective-permute-start.2) | collective-permute-done | bytes 131104 | tf_op jit(solution)/shard_map/ppermute | solution.py:308
  52.1 2.2 %collective-permute-done.1.refs_1_ = bf16[256,256]{1,0:T(8,128)(2,1)S(1)} collective-permute-done((bf16[256,256]{1,0:T(8,128)(2,1)S(1)}, bf16[256,256]{1,0:T(8,128)(2,1)S(1)}, u32[]{:S(2)}, u32[]{:S(2)}) %collective-permute-start.1) | collective-permute-done | bytes 131104 | tf_op jit(solution)/shard_map/ppermute | solution.py:308
  54.3 1.8 %collective-permute-done.refs_0_ = bf16[256,256]{1,0:T(8,128)(2,1)S(1)} collective-permute-done((bf16[256,256]{1,0:T(8,128)(2,1)S(1)}, bf16[256,256]{1,0:T(8,128)(2,1)S(1)}, u32[]{:S(2)}, u32[]{:S(2)}) %collective-permute-start) | collective-permute-done | bytes 131104 | tf_op jit(solution)/shard_map/ppermute | solution.py:308
  56.1 0.8 second_carry.1
  56.9 18.9 %all_to_all.22.in_ref = bf16[32,104,128]{2,1,0:T(8,128)(2,1)S(1)} all-to-all(bf16[32,104,128]{2,1,0:T(8,128)(2,1)S(1)} %bitcast.6), channel_id=1, replica_groups=mesh['sec'=32,'mpo'=4] {'sec'}, dimensions={0} | all-to-all | bytes 1703936 | tf_op jit(solution)/shard_map/all_to_all | solution.py:303
  75.8 0.6 second_mix.1
  76.4 17.9 %all_to_all.23 = bf16[32,48,256]{2,1,0:T(8,128)(2,1)S(1)} all-to-all(bf16[32,48,256]{2,1,0:T(8,128)(2,1)S(1)} %second_mix.1), channel_id=1, replica_groups=mesh['sec'=32,'mpo'=4] {'sec'}, dimensions={0} | all-to-all | bytes 1572864 | tf_op jit(solution)/shard_map/all_to_all | solution.py:303
  94.3 0.4 second_left.1
  94.7 0.7 collective-permute-start.3
  95.4 2.1 %collective-permute-start.4 = (bf16[64,256]{1,0:T(8,128)(2,1)S(1)}, bf16[64,256]{1,0:T(8,128)(2,1)S(1)}, u32[]{:S(2)}, u32[]{:S(2)}) collective-permute-start(bf16[64,256]{1,0:T(8,128)(2,1)S(1)} %get-tuple-element.32), channel_id=1, source_target_pairs={{0,1},{1,2},{2,3},{3,0},{4,5},{5,6},{6,7},{7,4},{8,9},{9,10},{10,1... | collective-permute-start | bytes 98312 | tf_op jit(solution)/shard_map/ppermute | solution.py:308
  97.5 1.2 %collective-permute-start.5 = (bf16[64,256]{1,0:T(8,128)(2,1)S(1)}, bf16[64,256]{1,0:T(8,128)(2,1)S(1)}, u32[]{:S(2)}, u32[]{:S(2)}) collective-permute-start(bf16[64,256]{1,0:T(8,128)(2,1)S(1)} %get-tuple-element.33), channel_id=1, source_target_pairs={{0,3},{1,0},{2,1},{3,2},{4,7},{5,4},{6,5},{7,6},{8,11},{9,8},{10,9... | collective-permute-start | bytes 98312 | tf_op jit(solution)/shard_map/ppermute | solution.py:308
  98.7 1.5 %collective-permute-done.3.refs_1_ = bf16[64,256]{1,0:T(8,128)(2,1)S(1)} collective-permute-done((bf16[64,256]{1,0:T(8,128)(2,1)S(1)}, bf16[64,256]{1,0:T(8,128)(2,1)S(1)}, u32[]{:S(2)}, u32[]{:S(2)}) %collective-permute-start.3) | collective-permute-done | bytes 32800 | tf_op jit(solution)/shard_map/ppermute | solution.py:308
  100.2 0.4 collective-permute-done.4.refs_2_
  100.6 0.8 collective-permute-done.5.refs_3_
  101.4 0.7 second_sum.1
  (2 shorter events, 0.0 us)
Async XLA Ops:
  25.3 18.7 %copy-start = (bf16[1,6,256,256]{3,2,1,0:T(8,128)(2,1)S(1)}, bf16[1,6,256,256]{3,2,1,0:T(8,128)(2,1)}, u32[]{:S(2)}) copy-start(bf16[1,6,256,256]{3,2,1,0:T(8,128)(2,1)} %left_ref.3) | copy-start | bytes 2359300
  44.4 7.7 %collective-permute-start.2 = (bf16[256,256]{1,0:T(8,128)(2,1)S(1)}, bf16[256,256]{1,0:T(8,128)(2,1)S(1)}, u32[]{:S(2)}, u32[]{:S(2)}) collective-permute-start(bf16[256,256]{1,0:T(8,128)(2,1)S(1)} %get-tuple-element.26), channel_id=1, source_target_pairs={{0,1},{1,2},{2,3},{3,0},{4,5},{5,6},{6,7},{7,4},{8,9},{9,10},{10,1... | collective-permute-start | bytes 393224 | tf_op jit(solution)/shard_map/ppermute | solution.py:308
  46.4 7.9 %collective-permute-start.1 = (bf16[256,256]{1,0:T(8,128)(2,1)S(1)}, bf16[256,256]{1,0:T(8,128)(2,1)S(1)}, u32[]{:S(2)}, u32[]{:S(2)}) collective-permute-start(bf16[256,256]{1,0:T(8,128)(2,1)S(1)} %get-tuple-element.26), channel_id=1, source_target_pairs={{0,3},{1,0},{2,1},{3,2},{4,7},{5,4},{6,5},{7,6},{8,11},{9,8},{10,9... | collective-permute-start | bytes 393224 | tf_op jit(solution)/shard_map/ppermute | solution.py:308
  48.6 7.5 %collective-permute-start = (bf16[256,256]{1,0:T(8,128)(2,1)S(1)}, bf16[256,256]{1,0:T(8,128)(2,1)S(1)}, u32[]{:S(2)}, u32[]{:S(2)}) collective-permute-start(bf16[256,256]{1,0:T(8,128)(2,1)S(1)} %get-tuple-element.26), channel_id=1, source_target_pairs={{0,2},{1,3},{2,0},{3,1},{4,6},{5,7},{6,4},{7,5},{8,10},{9,11},{10,... | collective-permute-start | bytes 393224 | tf_op jit(solution)/shard_map/ppermute | solution.py:308
  94.7 5.5 %collective-permute-start.3 = (bf16[64,256]{1,0:T(8,128)(2,1)S(1)}, bf16[64,256]{1,0:T(8,128)(2,1)S(1)}, u32[]{:S(2)}, u32[]{:S(2)}) collective-permute-start(bf16[64,256]{1,0:T(8,128)(2,1)S(1)} %get-tuple-element.31), channel_id=1, source_target_pairs={{0,2},{1,3},{2,0},{3,1},{4,6},{5,7},{6,4},{7,5},{8,10},{9,11},{10,... | collective-permute-start | bytes 98312 | tf_op jit(solution)/shard_map/ppermute | solution.py:308
  95.4 5.1 %collective-permute-start.4 = (bf16[64,256]{1,0:T(8,128)(2,1)S(1)}, bf16[64,256]{1,0:T(8,128)(2,1)S(1)}, u32[]{:S(2)}, u32[]{:S(2)}) collective-permute-start(bf16[64,256]{1,0:T(8,128)(2,1)S(1)} %get-tuple-element.32), channel_id=1, source_target_pairs={{0,1},{1,2},{2,3},{3,0},{4,5},{5,6},{6,7},{7,4},{8,9},{9,10},{10,1... | collective-permute-start | bytes 98312 | tf_op jit(solution)/shard_map/ppermute | solution.py:308
  97.5 3.9 %collective-permute-start.5 = (bf16[64,256]{1,0:T(8,128)(2,1)S(1)}, bf16[64,256]{1,0:T(8,128)(2,1)S(1)}, u32[]{:S(2)}, u32[]{:S(2)}) collective-permute-start(bf16[64,256]{1,0:T(8,128)(2,1)S(1)} %get-tuple-element.33), channel_id=1, source_target_pairs={{0,3},{1,0},{2,1},{3,2},{4,7},{5,4},{6,5},{7,6},{8,11},{9,8},{10,9... | collective-permute-start | bytes 98312 | tf_op jit(solution)/shard_map/ppermute | solution.py:308

commit v5 on v4

--- a/solution.py
+++ b/solution.py
@@ -17,7 +17,8 @@
 LANES = 128
 DATA_ROWS = HALF_TERMS * 2 * SLAB
 SIDE_ROWS = 8
-MIX = SECTORS * SLAB
+PART = 8
+MIX = SECTORS * PART
 EPSILON = 1e-06
 LIFT = 512.0
 
@@ -102,38 +103,40 @@
 
 def mix_with(weights_ref, in_ref, out_ref, scale):
     for place in range(HALF_TERMS):
-        parts = []
-        for side in range(2):
-            row = (place * 2 + side) * SLAB
-            parts.append(in_ref[:, row : row + SLAB, :].reshape(MIX, LANES))
-        mixed = jnp.dot(
-            weights_ref[place], jnp.concatenate(parts, axis=1), preferred_element_type=F32
-        )
-        if scale is not None:
-            mixed = jnp.where(scale > 0.0, mixed * scale, 0.0)
-        mixed = mixed.astype(BF16).reshape(SECTORS, SLAB, BLOCK)
-        out_ref[:, place * SLAB : (place + 1) * SLAB, :] = mixed
+        for start in range(0, SLAB, PART):
+            sides = []
+            for side in range(2):
+                row = (place * 2 + side) * SLAB + start
+                sides.append(in_ref[:, row : row + PART, :].reshape(MIX, LANES))
+            mixed = jnp.dot(
+                weights_ref[place], jnp.concatenate(sides, axis=1), preferred_element_type=F32
+            )
+            if scale is not None:
+                mixed = jnp.where(scale > 0.0, mixed * scale, 0.0)
+            row = place * SLAB + start
+            out_ref[:, row : row + PART, :] = mixed.astype(BF16).reshape(SECTORS, PART, BLOCK)
 
 
 def first_mix_kernel(in_ref, out_ref, weights_ref, wide_ref):
     counts = in_ref[:, DATA_ROWS:, :].reshape(SECTORS * SIDE_ROWS, LANES)
     sent_row = lax.broadcasted_iota(jnp.int32, (SECTORS * SIDE_ROWS, MIX), 0)
     mixed_row = lax.broadcasted_iota(jnp.int32, (SECTORS * SIDE_ROWS, MIX), 1)
-    spread = sent_row == mixed_row // SLAB * SIDE_ROWS
+    spread = sent_row == mixed_row // PART * SIDE_ROWS
     spread = jnp.where(spread, 1.0, 0.0).astype(BF16)
     wide_ref[...] = lax.dot_general(
         counts, spread, (((0,), (0,)), ((), ())), preferred_element_type=F32
     )
     same_row = (
-        lax.broadcasted_iota(jnp.int32, (SLAB, MIX), 0)
-        == lax.broadcasted_iota(jnp.int32, (SLAB, MIX), 1) % SLAB
+        lax.broadcasted_iota(jnp.int32, (PART, MIX), 0)
+        == lax.broadcasted_iota(jnp.int32, (PART, MIX), 1) % PART
     )
     same_row = jnp.where(same_row, 1.0, 0.0)
     for place in range(HALF_TERMS):
-        for target in range(SECTORS):
+        for target in range(0, SECTORS, 2):
             line = place * SECTORS + target
-            weights_ref[place, target * SLAB : (target + 1) * SLAB, :] = (
-                same_row * wide_ref[line : line + 1, :]
+            both = [same_row * wide_ref[line + k : line + k + 1, :] for k in range(2)]
+            weights_ref[place, target * PART : (target + 2) * PART, :] = jnp.concatenate(
+                both, axis=0
             ).astype(BF16)
     mix_with(weights_ref, in_ref, out_ref, None)
 
@@ -231,15 +234,14 @@
 
 
 def second_carry_kernel(live_ref, right_ref, own_ref, *refs):
-    *part_refs, out_ref, first_hbm, total, sem = refs
+    *part_refs, out_ref, share_ref, total = refs
     value = own_ref[...]
     for part_ref in part_refs:
         value += part_ref[...].astype(F32)
     value = live_only(value, 0, live_ref[:1, :1])
     total[...] = value
     first_row = pl.multiple_of(lax.axis_index("mpo") * SHARE, SHARE)
-    copy = pltpu.make_async_copy(total.at[pl.ds(first_row, SHARE), :], first_hbm.at[0], sem)
-    copy.start()
+    share_ref[...] = total[pl.ds(first_row, SHARE), :]
     mean = jnp.sum(value * value, keepdims=True) * (1.0 / (SECTORS * BLOCK * BLOCK))
     high = mean.astype(BF16)
     rest = jnp.where(mean < jnp.inf, mean - high.astype(F32), 0.0)
@@ -261,7 +263,6 @@
     for term in range(TERMS):
         carried = jnp.dot(both, right_ref[0, term], preferred_element_type=F32)
         store_carried(term, carried[:BLOCK] + carried[BLOCK:], out_ref)
-    copy.wait()
 
 
 def second_carry(live, right, own, parts):
@@ -269,33 +270,41 @@
         second_carry_kernel,
         out_shape=(
             jax.ShapeDtypeStruct((SLABS, 2, DATA_ROWS + SIDE_ROWS, LANES), BF16),
-            jax.ShapeDtypeStruct((1, SHARE, BLOCK), F32),
+            jax.ShapeDtypeStruct((SHARE, BLOCK), F32),
         ),
         in_specs=[VMEM] * (GROUPS + 2),
-        out_specs=(VMEM, HBM),
-        scratch_shapes=[pltpu.VMEM((BLOCK, BLOCK), F32), pltpu.SemaphoreType.DMA],
+        out_specs=(VMEM, VMEM),
+        scratch_shapes=[pltpu.VMEM((BLOCK, BLOCK), F32)],
         compiler_params=PARAMS,
         name="second_carry",
     )(live, right, own, *parts)
 
 
-def second_sum_kernel(live_ref, *refs):
-    *part_refs, out_ref = refs
+def outputs_kernel(live_ref, share_ref, *refs):
+    *part_refs, first_hbm, second_hbm, total, sems = refs
+    first_copy = pltpu.make_async_copy(share_ref, first_hbm.at[0], sems.at[0])
+    first_copy.start()
     value = part_refs[0][...]
     for part_ref in part_refs[1:]:
         value += part_ref[...].astype(F32)
-    out_ref[0] = live_only(value, lax.axis_index("mpo") * SHARE, live_ref[:1, :1])
-
-
-def second_sum(live, parts):
-    return pl.pallas_call(
-        second_sum_kernel,
-        out_shape=jax.ShapeDtypeStruct((1, SHARE, BLOCK), F32),
-        in_specs=[VMEM] * (GROUPS + 1),
-        out_specs=VMEM,
-        compiler_params=PARAMS,
-        name="second_sum",
-    )(live, *parts)
+    total[...] = live_only(value, lax.axis_index("mpo") * SHARE, live_ref[:1, :1])
+    second_copy = pltpu.make_async_copy(total, second_hbm.at[0], sems.at[1])
+    second_copy.start()
+    first_copy.wait()
+    second_copy.wait()
+
+
+def outputs(live, share, parts):
+    result = jax.ShapeDtypeStruct((1, SHARE, BLOCK), F32)
+    return pl.pallas_call(
+        outputs_kernel,
+        out_shape=(result, result),
+        in_specs=[VMEM] * (GROUPS + 2),
+        out_specs=(HBM, HBM),
+        scratch_shapes=[pltpu.VMEM((SHARE, BLOCK), F32), pltpu.SemaphoreType.DMA((2,))],
+        compiler_params=PARAMS,
+        name="outputs",
+    )(live, share, *parts)
 
 
 def exchange(messages):
@@ -314,12 +323,11 @@
     mixed, weights = first_mix(exchange(carried))
     own, sent = first_left(exchange(mixed), left_env)
     parts = [shift(sent, step) for step in (2, 3, 1)]
-    carried, first_product = second_carry(live, fetched[0], own, parts)
+    carried, share = second_carry(live, fetched[0], own, parts)
     mixed = second_mix(exchange(carried), weights)
     parts = second_left(exchange(mixed), left_env)
     parts = [parts[0]] + [shift(parts[step], step) for step in (2, 1, 3)]
-    second_product = second_sum(live, parts)
-    return (first_product, second_product)
+    return outputs(live, share, parts)
 
 
 def solution(mesh):

time: 102 us -> 102 us (level)
  no operation moved by 1% of the time
where the time goes in v5:
time: 102 us
  blocking collectives  77.3 us (76%)
  starting transfers between devices  9.94 us (10%)
  waiting for transfers between devices  8.47 us (8%)
  Pallas kernels  4.64 us (5%)
  between operations  1.34 us (1%)
    all_to_all x4, blocking collectives, exchange(): lax.all_to_all(messages, 'sec', split_axis=0, concat_axis=0, tiled=True)  77.3 us
    ppermute x6, starting transfers between devices, shift(): return lax.ppermute(value, 'mpo', pairs)  9.94 us
    ppermute x6, waiting for transfers between devices, shift(): return lax.ppermute(value, 'mpo', pairs)  8.47 us
  transfers between devices with their start and end apart: 6, of which 6 were waited for; matrix products, arithmetic and copies ran while one was open for 0% of the time, Pallas kernels for 0%

profile of v5, /device:TPU:0, one launch (start us, length us, event | category | flops | bytes accessed | tf_op | source)
XLA Modules:
  0.0 101.7 jit_solution(3537237470052211232)
XLA Ops:
  1.3 1.2 %fetch.1 = (bf16[1,6,256,256]{3,2,1,0:T(8,128)(2,1)S(1)}, bf16[1,256,256]{2,1,0:T(8,128)(2,1)S(1)}, s32[1,32]{1,0:T(1,128)S(1)}, s32[1,32]{1,0:T(1,128)S(1)}) custom-call(bf16[1,6,256,256]{3,2,1,0:T(8,128)(2,1)} %refs_0_.1, bf16[1,256,256]{2,1,0:T(8,128)(2,1)} %refs_1_.1, s32[1,32]{1,0:T(1,128)} %refs_2_.1, s32[1,32]{1,0:T(1,128)} %refs_3_.1), custom_call_target="tpu_custom_call" | custom-call | tf_op jit(solution)/shard_map/fetch/pallas_call | solution.py:56
  2.5 0.4 first_carry.1
  2.9 22.4 %all_to_all.20.in_ref = bf16[32,104,128]{2,1,0:T(8,128)(2,1)S(1)} all-to-all(bf16[32,104,128]{2,1,0:T(8,128)(2,1)S(1)} %bitcast.7), channel_id=1, replica_groups=mesh['sec'=32,'mpo'=4] {'sec'}, dimensions={0} | all-to-all | bytes 1703936 | tf_op jit(solution)/shard_map/all_to_all | solution.py:312
  25.3 0.5 first_mix.1
  25.8 18.1 %all_to_all.21 = bf16[32,48,256]{2,1,0:T(8,128)(2,1)S(1)} all-to-all(bf16[32,48,256]{2,1,0:T(8,128)(2,1)S(1)} %get-tuple-element.24), channel_id=1, replica_groups=mesh['sec'=32,'mpo'=4] {'sec'}, dimensions={0} | all-to-all | bytes 1572864 | tf_op jit(solution)/shard_map/all_to_all | solution.py:312
  43.9 0.4 first_left.1
  44.3 2.0 %collective-permute-start.2 = (bf16[256,256]{1,0:T(8,128)(2,1)S(1)}, bf16[256,256]{1,0:T(8,128)(2,1)S(1)}, u32[]{:S(2)}, u32[]{:S(2)}) collective-permute-start(bf16[256,256]{1,0:T(8,128)(2,1)S(1)} %get-tuple-element.26), channel_id=1, source_target_pairs={{0,1},{1,2},{2,3},{3,0},{4,5},{5,6},{6,7},{7,4},{8,9},{9,10},{10,1... | collective-permute-start | bytes 393224 | tf_op jit(solution)/shard_map/ppermute | solution.py:317
  46.3 2.2 %collective-permute-start.1 = (bf16[256,256]{1,0:T(8,128)(2,1)S(1)}, bf16[256,256]{1,0:T(8,128)(2,1)S(1)}, u32[]{:S(2)}, u32[]{:S(2)}) collective-permute-start(bf16[256,256]{1,0:T(8,128)(2,1)S(1)} %get-tuple-element.26), channel_id=1, source_target_pairs={{0,3},{1,0},{2,1},{3,2},{4,7},{5,4},{6,5},{7,6},{8,11},{9,8},{10,9... | collective-permute-start | bytes 393224 | tf_op jit(solution)/shard_map/ppermute | solution.py:317
  48.5 1.8 %collective-permute-start = (bf16[256,256]{1,0:T(8,128)(2,1)S(1)}, bf16[256,256]{1,0:T(8,128)(2,1)S(1)}, u32[]{:S(2)}, u32[]{:S(2)}) collective-permute-start(bf16[256,256]{1,0:T(8,128)(2,1)S(1)} %get-tuple-element.26), channel_id=1, source_target_pairs={{0,2},{1,3},{2,0},{3,1},{4,6},{5,7},{6,4},{7,5},{8,10},{9,11},{10,... | collective-permute-start | bytes 393224 | tf_op jit(solution)/shard_map/ppermute | solution.py:317
  50.2 1.7 %collective-permute-done.2.refs_2_ = bf16[256,256]{1,0:T(8,128)(2,1)S(1)} collective-permute-done((bf16[256,256]{1,0:T(8,128)(2,1)S(1)}, bf16[256,256]{1,0:T(8,128)(2,1)S(1)}, u32[]{:S(2)}, u32[]{:S(2)}) %collective-permute-start.2) | collective-permute-done | bytes 131104 | tf_op jit(solution)/shard_map/ppermute | solution.py:317
  52.0 2.2 %collective-permute-done.1.refs_1_ = bf16[256,256]{1,0:T(8,128)(2,1)S(1)} collective-permute-done((bf16[256,256]{1,0:T(8,128)(2,1)S(1)}, bf16[256,256]{1,0:T(8,128)(2,1)S(1)}, u32[]{:S(2)}, u32[]{:S(2)}) %collective-permute-start.1) | collective-permute-done | bytes 131104 | tf_op jit(solution)/shard_map/ppermute | solution.py:317
  54.2 1.8 %collective-permute-done.refs_0_ = bf16[256,256]{1,0:T(8,128)(2,1)S(1)} collective-permute-done((bf16[256,256]{1,0:T(8,128)(2,1)S(1)}, bf16[256,256]{1,0:T(8,128)(2,1)S(1)}, u32[]{:S(2)}, u32[]{:S(2)}) %collective-permute-start) | collective-permute-done | bytes 131104 | tf_op jit(solution)/shard_map/ppermute | solution.py:317
  56.0 0.6 second_carry.1
  56.6 18.9 %all_to_all.22.in_ref = bf16[32,104,128]{2,1,0:T(8,128)(2,1)S(1)} all-to-all(bf16[32,104,128]{2,1,0:T(8,128)(2,1)S(1)} %bitcast.6), channel_id=1, replica_groups=mesh['sec'=32,'mpo'=4] {'sec'}, dimensions={0} | all-to-all | bytes 1703936 | tf_op jit(solution)/shard_map/all_to_all | solution.py:312
  75.6 0.4 second_mix.1
  76.0 17.9 %all_to_all.23 = bf16[32,48,256]{2,1,0:T(8,128)(2,1)S(1)} all-to-all(bf16[32,48,256]{2,1,0:T(8,128)(2,1)S(1)} %second_mix.1), channel_id=1, replica_groups=mesh['sec'=32,'mpo'=4] {'sec'}, dimensions={0} | all-to-all | bytes 1572864 | tf_op jit(solution)/shard_map/all_to_all | solution.py:312
  93.9 0.4 second_left.1
  94.3 0.7 collective-permute-start.3
  95.0 2.1 %collective-permute-start.4 = (bf16[64,256]{1,0:T(8,128)(2,1)S(1)}, bf16[64,256]{1,0:T(8,128)(2,1)S(1)}, u32[]{:S(2)}, u32[]{:S(2)}) collective-permute-start(bf16[64,256]{1,0:T(8,128)(2,1)S(1)} %get-tuple-element.32), channel_id=1, source_target_pairs={{0,1},{1,2},{2,3},{3,0},{4,5},{5,6},{6,7},{7,4},{8,9},{9,10},{10,1... | collective-permute-start | bytes 98312 | tf_op jit(solution)/shard_map/ppermute | solution.py:317
  97.1 1.2 %collective-permute-start.5 = (bf16[64,256]{1,0:T(8,128)(2,1)S(1)}, bf16[64,256]{1,0:T(8,128)(2,1)S(1)}, u32[]{:S(2)}, u32[]{:S(2)}) collective-permute-start(bf16[64,256]{1,0:T(8,128)(2,1)S(1)} %get-tuple-element.33), channel_id=1, source_target_pairs={{0,3},{1,0},{2,1},{3,2},{4,7},{5,4},{6,5},{7,6},{8,11},{9,8},{10,9... | collective-permute-start | bytes 98312 | tf_op jit(solution)/shard_map/ppermute | solution.py:317
  98.3 1.5 %collective-permute-done.3.refs_1_ = bf16[64,256]{1,0:T(8,128)(2,1)S(1)} collective-permute-done((bf16[64,256]{1,0:T(8,128)(2,1)S(1)}, bf16[64,256]{1,0:T(8,128)(2,1)S(1)}, u32[]{:S(2)}, u32[]{:S(2)}) %collective-permute-start.3) | collective-permute-done | bytes 32800 | tf_op jit(solution)/shard_map/ppermute | solution.py:317
  99.8 0.4 collective-permute-done.4.refs_2_
  100.2 0.9 collective-permute-done.5.refs_3_
  101.0 0.7 outputs.1
  (2 shorter events, 0.0 us)
Async XLA Ops:
  25.8 18.1 %copy-start = (bf16[1,6,256,256]{3,2,1,0:T(8,128)(2,1)S(1)}, bf16[1,6,256,256]{3,2,1,0:T(8,128)(2,1)}, u32[]{:S(2)}) copy-start(bf16[1,6,256,256]{3,2,1,0:T(8,128)(2,1)} %left_ref.3) | copy-start | bytes 2359300
  44.3 7.7 %collective-permute-start.2 = (bf16[256,256]{1,0:T(8,128)(2,1)S(1)}, bf16[256,256]{1,0:T(8,128)(2,1)S(1)}, u32[]{:S(2)}, u32[]{:S(2)}) collective-permute-start(bf16[256,256]{1,0:T(8,128)(2,1)S(1)} %get-tuple-element.26), channel_id=1, source_target_pairs={{0,1},{1,2},{2,3},{3,0},{4,5},{5,6},{6,7},{7,4},{8,9},{9,10},{10,1... | collective-permute-start | bytes 393224 | tf_op jit(solution)/shard_map/ppermute | solution.py:317
  46.3 7.9 %collective-permute-start.1 = (bf16[256,256]{1,0:T(8,128)(2,1)S(1)}, bf16[256,256]{1,0:T(8,128)(2,1)S(1)}, u32[]{:S(2)}, u32[]{:S(2)}) collective-permute-start(bf16[256,256]{1,0:T(8,128)(2,1)S(1)} %get-tuple-element.26), channel_id=1, source_target_pairs={{0,3},{1,0},{2,1},{3,2},{4,7},{5,4},{6,5},{7,6},{8,11},{9,8},{10,9... | collective-permute-start | bytes 393224 | tf_op jit(solution)/shard_map/ppermute | solution.py:317
  48.5 7.5 %collective-permute-start = (bf16[256,256]{1,0:T(8,128)(2,1)S(1)}, bf16[256,256]{1,0:T(8,128)(2,1)S(1)}, u32[]{:S(2)}, u32[]{:S(2)}) collective-permute-start(bf16[256,256]{1,0:T(8,128)(2,1)S(1)} %get-tuple-element.26), channel_id=1, source_target_pairs={{0,2},{1,3},{2,0},{3,1},{4,6},{5,7},{6,4},{7,5},{8,10},{9,11},{10,... | collective-permute-start | bytes 393224 | tf_op jit(solution)/shard_map/ppermute | solution.py:317
  94.3 5.5 %collective-permute-start.3 = (bf16[64,256]{1,0:T(8,128)(2,1)S(1)}, bf16[64,256]{1,0:T(8,128)(2,1)S(1)}, u32[]{:S(2)}, u32[]{:S(2)}) collective-permute-start(bf16[64,256]{1,0:T(8,128)(2,1)S(1)} %get-tuple-element.31), channel_id=1, source_target_pairs={{0,2},{1,3},{2,0},{3,1},{4,6},{5,7},{6,4},{7,5},{8,10},{9,11},{10,... | collective-permute-start | bytes 98312 | tf_op jit(solution)/shard_map/ppermute | solution.py:317
  95.0 5.2 %collective-permute-start.4 = (bf16[64,256]{1,0:T(8,128)(2,1)S(1)}, bf16[64,256]{1,0:T(8,128)(2,1)S(1)}, u32[]{:S(2)}, u32[]{:S(2)}) collective-permute-start(bf16[64,256]{1,0:T(8,128)(2,1)S(1)} %get-tuple-element.32), channel_id=1, source_target_pairs={{0,1},{1,2},{2,3},{3,0},{4,5},{5,6},{6,7},{7,4},{8,9},{9,10},{10,1... | collective-permute-start | bytes 98312 | tf_op jit(solution)/shard_map/ppermute | solution.py:317
  97.1 3.9 %collective-permute-start.5 = (bf16[64,256]{1,0:T(8,128)(2,1)S(1)}, bf16[64,256]{1,0:T(8,128)(2,1)S(1)}, u32[]{:S(2)}, u32[]{:S(2)}) collective-permute-start(bf16[64,256]{1,0:T(8,128)(2,1)S(1)} %get-tuple-element.33), channel_id=1, source_target_pairs={{0,3},{1,0},{2,1},{3,2},{4,7},{5,4},{6,5},{7,6},{8,11},{9,8},{10,9... | collective-permute-start | bytes 98312 | tf_op jit(solution)/shard_map/ppermute | solution.py:317

commit v6 on v5

--- a/solution.py
+++ b/solution.py
@@ -242,6 +242,13 @@
     total[...] = value
     first_row = pl.multiple_of(lax.axis_index("mpo") * SHARE, SHARE)
     share_ref[...] = total[pl.ds(first_row, SHARE), :]
+    lifted = value * LIFT
+    upper = lifted.astype(BF16)
+    lower = (lifted - upper.astype(F32)).astype(BF16)
+    both = jnp.concatenate([upper, lower], axis=0)
+    for term in range(TERMS):
+        carried = jnp.dot(both, right_ref[0, term], preferred_element_type=F32)
+        store_carried(term, carried[:BLOCK] + carried[BLOCK:], out_ref)
     mean = jnp.sum(value * value, keepdims=True) * (1.0 / (SECTORS * BLOCK * BLOCK))
     high = mean.astype(BF16)
     rest = jnp.where(mean < jnp.inf, mean - high.astype(F32), 0.0)
@@ -256,13 +263,6 @@
     for slab in range(SLABS):
         for half in range(2):
             out_ref[slab, half, DATA_ROWS:, :] = pieces
-    lifted = value * LIFT
-    upper = lifted.astype(BF16)
-    lower = (lifted - upper.astype(F32)).astype(BF16)
-    both = jnp.concatenate([upper, lower], axis=0)
-    for term in range(TERMS):
-        carried = jnp.dot(both, right_ref[0, term], preferred_element_type=F32)
-        store_carried(term, carried[:BLOCK] + carried[BLOCK:], out_ref)
 
 
 def second_carry(live, right, own, parts):
@@ -317,12 +317,22 @@
     return lax.ppermute(value, "mpo", pairs)
 
 
+def shift_both_ways(value, step):
+    pairs = []
+    for sector in range(SECTORS):
+        ahead = step if sector % 2 == 0 else GROUPS - step
+        for group in range(GROUPS):
+            target = (group + ahead) % GROUPS
+            pairs.append((sector * GROUPS + group, sector * GROUPS + target))
+    return lax.ppermute(value, ("sec", "mpo"), pairs)
+
+
 def body(wavefunction, block_dims, left_env, right_env, task_left, task_term):
     fetched = fetch(right_env, wavefunction, task_left, task_term)
     carried, live = first_carry(block_dims, fetched)
     mixed, weights = first_mix(exchange(carried))
     own, sent = first_left(exchange(mixed), left_env)
-    parts = [shift(sent, step) for step in (2, 3, 1)]
+    parts = [shift_both_ways(sent, step) for step in (2, 3, 1)]
     carried, share = second_carry(live, fetched[0], own, parts)
     mixed = second_mix(exchange(carried), weights)
     parts = second_left(exchange(mixed), left_env)

time: 102 us -> 102 us (level)
    ppermute x0 -> x3, starting transfers between devices: none -> 5.96 us  [shift_both_ways(): return lax.ppermute(value, ('sec', 'mpo'), pairs)]
    ppermute x6 -> x3, starting transfers between devices: 9.94 us -> 4.07 us  [shift(): return lax.ppermute(value, 'mpo', pairs)]
    ppermute x0 -> x3, waiting for transfers between devices: none -> 5.85 us  [shift_both_ways(): return lax.ppermute(value, ('sec', 'mpo'), pairs)]
    ppermute x6 -> x3, waiting for transfers between devices: 8.47 us -> 2.65 us  [shift(): return lax.ppermute(value, 'mpo', pairs)]
  transfers between devices with their start and end apart: 6 -> 6, of which waited for: 6 -> 5; matrix products, arithmetic and copies ran while one was open for 0% -> 0% of each run, Pallas kernels for 0% -> 0%
where the time goes in v6:
time: 102 us
  blocking collectives  77.2 us (76%)
  starting transfers between devices  10 us (10%)
  waiting for transfers between devices  8.5 us (8%)
  Pallas kernels  4.63 us (5%)
  between operations  1.34 us (1%)
    all_to_all x4, blocking collectives, exchange(): lax.all_to_all(messages, 'sec', split_axis=0, concat_axis=0, tiled=True)  77.2 us
    ppermute x3, starting transfers between devices, shift_both_ways(): return lax.ppermute(value, ('sec', 'mpo'), pairs)  5.96 us
    ppermute x3, waiting for transfers between devices, shift_both_ways(): return lax.ppermute(value, ('sec', 'mpo'), pairs)  5.85 us
    ppermute x3, starting transfers between devices, shift(): return lax.ppermute(value, 'mpo', pairs)  4.07 us
    ppermute x3, waiting for transfers between devices, shift(): return lax.ppermute(value, 'mpo', pairs)  2.65 us
  transfers between devices with their start and end apart: 6, of which 5 were waited for; matrix products, arithmetic and copies ran while one was open for 0% of the time, Pallas kernels for 0%

profile of v6, /device:TPU:0, one launch (start us, length us, event | category | flops | bytes accessed | tf_op | source)
XLA Modules:
  0.0 101.7 jit_solution(14552197193065051758)
XLA Ops:
  1.3 1.2 %fetch.1 = (bf16[1,6,256,256]{3,2,1,0:T(8,128)(2,1)S(1)}, bf16[1,256,256]{2,1,0:T(8,128)(2,1)S(1)}, s32[1,32]{1,0:T(1,128)S(1)}, s32[1,32]{1,0:T(1,128)S(1)}) custom-call(bf16[1,6,256,256]{3,2,1,0:T(8,128)(2,1)} %refs_0_.1, bf16[1,256,256]{2,1,0:T(8,128)(2,1)} %refs_1_.1, s32[1,32]{1,0:T(1,128)} %refs_2_.1, s32[1,32]{1,0:T(1,128)} %refs_3_.1), custom_call_target="tpu_custom_call" | custom-call | tf_op jit(solution)/shard_map/fetch/pallas_call | solution.py:56
  2.5 0.4 first_carry.1
  2.9 22.4 %all_to_all.20.in_ref = bf16[32,104,128]{2,1,0:T(8,128)(2,1)S(1)} all-to-all(bf16[32,104,128]{2,1,0:T(8,128)(2,1)S(1)} %bitcast.7), channel_id=1, replica_groups=mesh['sec'=32,'mpo'=4] {'sec'}, dimensions={0} | all-to-all | bytes 1703936 | tf_op jit(solution)/shard_map/all_to_all | solution.py:312
  25.3 0.5 first_mix.1
  25.8 0.0 copy-start
  25.8 18.1 %all_to_all.21 = bf16[32,48,256]{2,1,0:T(8,128)(2,1)S(1)} all-to-all(bf16[32,48,256]{2,1,0:T(8,128)(2,1)S(1)} %get-tuple-element.24), channel_id=1, replica_groups=mesh['sec'=32,'mpo'=4] {'sec'}, dimensions={0} | all-to-all | bytes 1572864 | tf_op jit(solution)/shard_map/all_to_all | solution.py:312
  43.9 0.4 first_left.1
  44.3 2.0 %collective-permute-start.2 = (bf16[256,256]{1,0:T(8,128)(2,1)S(1)}, bf16[256,256]{1,0:T(8,128)(2,1)S(1)}, u32[]{:S(2)}, u32[]{:S(2)}) collective-permute-start(bf16[256,256]{1,0:T(8,128)(2,1)S(1)} %get-tuple-element.26), channel_id=1, source_target_pairs={{0,1},{1,2},{2,3},{3,0},{4,7},{5,4},{6,5},{7,6},{8,9},{9,10},{10,1... | collective-permute-start | bytes 393224 | tf_op jit(solution)/shard_map/ppermute | solution.py:327
  46.3 2.2 %collective-permute-start.1 = (bf16[256,256]{1,0:T(8,128)(2,1)S(1)}, bf16[256,256]{1,0:T(8,128)(2,1)S(1)}, u32[]{:S(2)}, u32[]{:S(2)}) collective-permute-start(bf16[256,256]{1,0:T(8,128)(2,1)S(1)} %get-tuple-element.26), channel_id=1, source_target_pairs={{0,3},{1,0},{2,1},{3,2},{4,5},{5,6},{6,7},{7,4},{8,11},{9,8},{10,9... | collective-permute-start | bytes 393224 | tf_op jit(solution)/shard_map/ppermute | solution.py:327
  48.5 1.8 %collective-permute-start = (bf16[256,256]{1,0:T(8,128)(2,1)S(1)}, bf16[256,256]{1,0:T(8,128)(2,1)S(1)}, u32[]{:S(2)}, u32[]{:S(2)}) collective-permute-start(bf16[256,256]{1,0:T(8,128)(2,1)S(1)} %get-tuple-element.26), channel_id=1, source_target_pairs={{0,2},{1,3},{2,0},{3,1},{4,6},{5,7},{6,4},{7,5},{8,10},{9,11},{10,... | collective-permute-start | bytes 393224 | tf_op jit(solution)/shard_map/ppermute | solution.py:327
  50.2 1.1 %collective-permute-done.2.refs_2_ = bf16[256,256]{1,0:T(8,128)(2,1)S(1)} collective-permute-done((bf16[256,256]{1,0:T(8,128)(2,1)S(1)}, bf16[256,256]{1,0:T(8,128)(2,1)S(1)}, u32[]{:S(2)}, u32[]{:S(2)}) %collective-permute-start.2) | collective-permute-done | bytes 131104 | tf_op jit(solution)/shard_map/ppermute | solution.py:327
  51.3 4.8 %collective-permute-done.refs_0_ = bf16[256,256]{1,0:T(8,128)(2,1)S(1)} collective-permute-done((bf16[256,256]{1,0:T(8,128)(2,1)S(1)}, bf16[256,256]{1,0:T(8,128)(2,1)S(1)}, u32[]{:S(2)}, u32[]{:S(2)}) %collective-permute-start) | collective-permute-done | bytes 131104 | tf_op jit(solution)/shard_map/ppermute | solution.py:327
  56.1 0.6 second_carry.1
  56.7 18.8 %all_to_all.22.in_ref = bf16[32,104,128]{2,1,0:T(8,128)(2,1)S(1)} all-to-all(bf16[32,104,128]{2,1,0:T(8,128)(2,1)S(1)} %bitcast.6), channel_id=1, replica_groups=mesh['sec'=32,'mpo'=4] {'sec'}, dimensions={0} | all-to-all | bytes 1703936 | tf_op jit(solution)/shard_map/all_to_all | solution.py:312
  75.5 0.4 second_mix.1
  76.0 17.9 %all_to_all.23 = bf16[32,48,256]{2,1,0:T(8,128)(2,1)S(1)} all-to-all(bf16[32,48,256]{2,1,0:T(8,128)(2,1)S(1)} %second_mix.1), channel_id=1, replica_groups=mesh['sec'=32,'mpo'=4] {'sec'}, dimensions={0} | all-to-all | bytes 1572864 | tf_op jit(solution)/shard_map/all_to_all | solution.py:312
  93.9 0.4 second_left.1
  94.3 0.8 collective-permute-start.3
  95.1 2.0 %collective-permute-start.4 = (bf16[64,256]{1,0:T(8,128)(2,1)S(1)}, bf16[64,256]{1,0:T(8,128)(2,1)S(1)}, u32[]{:S(2)}, u32[]{:S(2)}) collective-permute-start(bf16[64,256]{1,0:T(8,128)(2,1)S(1)} %get-tuple-element.32), channel_id=1, source_target_pairs={{0,1},{1,2},{2,3},{3,0},{4,5},{5,6},{6,7},{7,4},{8,9},{9,10},{10,1... | collective-permute-start | bytes 98312 | tf_op jit(solution)/shard_map/ppermute | solution.py:317
  97.1 1.3 %collective-permute-start.5 = (bf16[64,256]{1,0:T(8,128)(2,1)S(1)}, bf16[64,256]{1,0:T(8,128)(2,1)S(1)}, u32[]{:S(2)}, u32[]{:S(2)}) collective-permute-start(bf16[64,256]{1,0:T(8,128)(2,1)S(1)} %get-tuple-element.33), channel_id=1, source_target_pairs={{0,3},{1,0},{2,1},{3,2},{4,7},{5,4},{6,5},{7,6},{8,11},{9,8},{10,9... | collective-permute-start | bytes 98312 | tf_op jit(solution)/shard_map/ppermute | solution.py:317
  98.4 1.6 %collective-permute-done.3.refs_1_ = bf16[64,256]{1,0:T(8,128)(2,1)S(1)} collective-permute-done((bf16[64,256]{1,0:T(8,128)(2,1)S(1)}, bf16[64,256]{1,0:T(8,128)(2,1)S(1)}, u32[]{:S(2)}, u32[]{:S(2)}) %collective-permute-start.3) | collective-permute-done | bytes 32800 | tf_op jit(solution)/shard_map/ppermute | solution.py:317
  100.0 0.3 collective-permute-done.4.refs_2_
  100.3 0.7 collective-permute-done.5.refs_3_
  101.0 0.7 outputs.1
  (2 shorter events, 0.0 us)
Async XLA Ops:
  25.8 18.1 %copy-start = (bf16[1,6,256,256]{3,2,1,0:T(8,128)(2,1)S(1)}, bf16[1,6,256,256]{3,2,1,0:T(8,128)(2,1)}, u32[]{:S(2)}) copy-start(bf16[1,6,256,256]{3,2,1,0:T(8,128)(2,1)} %left_ref.3) | copy-start | bytes 2359300
  44.3 7.1 %collective-permute-start.2 = (bf16[256,256]{1,0:T(8,128)(2,1)S(1)}, bf16[256,256]{1,0:T(8,128)(2,1)S(1)}, u32[]{:S(2)}, u32[]{:S(2)}) collective-permute-start(bf16[256,256]{1,0:T(8,128)(2,1)S(1)} %get-tuple-element.26), channel_id=1, source_target_pairs={{0,1},{1,2},{2,3},{3,0},{4,7},{5,4},{6,5},{7,6},{8,9},{9,10},{10,1... | collective-permute-start | bytes 393224 | tf_op jit(solution)/shard_map/ppermute | solution.py:327
  46.3 5.1 %collective-permute-start.1 = (bf16[256,256]{1,0:T(8,128)(2,1)S(1)}, bf16[256,256]{1,0:T(8,128)(2,1)S(1)}, u32[]{:S(2)}, u32[]{:S(2)}) collective-permute-start(bf16[256,256]{1,0:T(8,128)(2,1)S(1)} %get-tuple-element.26), channel_id=1, source_target_pairs={{0,3},{1,0},{2,1},{3,2},{4,5},{5,6},{6,7},{7,4},{8,11},{9,8},{10,9... | collective-permute-start | bytes 393224 | tf_op jit(solution)/shard_map/ppermute | solution.py:327
  48.5 7.6 %collective-permute-start = (bf16[256,256]{1,0:T(8,128)(2,1)S(1)}, bf16[256,256]{1,0:T(8,128)(2,1)S(1)}, u32[]{:S(2)}, u32[]{:S(2)}) collective-permute-start(bf16[256,256]{1,0:T(8,128)(2,1)S(1)} %get-tuple-element.26), channel_id=1, source_target_pairs={{0,2},{1,3},{2,0},{3,1},{4,6},{5,7},{6,4},{7,5},{8,10},{9,11},{10,... | collective-permute-start | bytes 393224 | tf_op jit(solution)/shard_map/ppermute | solution.py:327
  94.3 5.7 %collective-permute-start.3 = (bf16[64,256]{1,0:T(8,128)(2,1)S(1)}, bf16[64,256]{1,0:T(8,128)(2,1)S(1)}, u32[]{:S(2)}, u32[]{:S(2)}) collective-permute-start(bf16[64,256]{1,0:T(8,128)(2,1)S(1)} %get-tuple-element.31), channel_id=1, source_target_pairs={{0,2},{1,3},{2,0},{3,1},{4,6},{5,7},{6,4},{7,5},{8,10},{9,11},{10,... | collective-permute-start | bytes 98312 | tf_op jit(solution)/shard_map/ppermute | solution.py:317
  95.1 5.2 %collective-permute-start.4 = (bf16[64,256]{1,0:T(8,128)(2,1)S(1)}, bf16[64,256]{1,0:T(8,128)(2,1)S(1)}, u32[]{:S(2)}, u32[]{:S(2)}) collective-permute-start(bf16[64,256]{1,0:T(8,128)(2,1)S(1)} %get-tuple-element.32), channel_id=1, source_target_pairs={{0,1},{1,2},{2,3},{3,0},{4,5},{5,6},{6,7},{7,4},{8,9},{9,10},{10,1... | collective-permute-start | bytes 98312 | tf_op jit(solution)/shard_map/ppermute | solution.py:317
  97.1 3.9 %collective-permute-start.5 = (bf16[64,256]{1,0:T(8,128)(2,1)S(1)}, bf16[64,256]{1,0:T(8,128)(2,1)S(1)}, u32[]{:S(2)}, u32[]{:S(2)}) collective-permute-start(bf16[64,256]{1,0:T(8,128)(2,1)S(1)} %get-tuple-element.33), channel_id=1, source_target_pairs={{0,3},{1,0},{2,1},{3,2},{4,7},{5,4},{6,5},{7,6},{8,11},{9,8},{10,9... | collective-permute-start | bytes 98312 | tf_op jit(solution)/shard_map/ppermute | solution.py:317
